TPU v7x, 256 devices: a whole 4x4x8 slice. The times are simulated.
256 devices in a mesh: blk: 32 (over z, x_lo, core), uly: 8 (over y, x_hi).
Axes of the slice: x: 4 (x_hi: 2, x_lo: 2; x = x_hi * 2 + x_lo), y: 4, z: 8, core: 2. Of those that a mesh axis runs over, the one named last changes fastest.
Arguments:
- queries: bfloat16 [4096, 5120], P(('blk', 'uly')), may hold values from -120 to 120
- keys: bfloat16 [4096, 5120], P(('blk', 'uly')), may hold values from -6.5 to 6.5
- values: bfloat16 [4096, 5120], P(('blk', 'uly')), may hold values from -16 to 16
- block_lists: int32 [32, 12], P('blk'), may hold values from 0 to 31, as said below
- block_counts: int32 [32], P('blk'), may hold values from 4 to 12, as said below
- out_weight: bfloat16 [5120, 5120], P('uly', 'blk'), may hold values from -0.078125 to 0.078125
- out_bias: float32 [5120], replicated, may hold values from -1.8 to 1.8
- out_gate: float32 [5120], replicated, may hold values from 0.5 to 1.5
Outputs:
- branch_out: bfloat16 [4096, 5120], P(('blk', 'uly'))
Inputs may be any that keep to these rules, and one draw needn't show every extreme that they name: `block_lists`: row i lists 12 distinct key-block numbers; its first entry is i itself; entries at slots block_counts[i] and beyond are ignored. `block_counts`: some query block uses all 12 slots.
All inputs are finite; a program needn't handle non-finite values.
Results may differ from a plain program's by a relative error of at most 0.015.
Values may be sent and summed in bfloat16 or wider, within the bound.
A program may use at most 128 MiB of HBM per device.

v0:
```python
import jax
import jax.numpy as jnp
from jax import lax
from jax.sharding import PartitionSpec as P

HEAD_DIM = 128
BLOCK = 128


def body(queries, keys, values, block_lists, block_counts, out_weight, out_bias, out_gate):
    q_part, k_part, v_part = (
        lax.all_to_all(queries, "uly", split_axis=1, concat_axis=0, tiled=True),
        lax.all_to_all(keys, "uly", split_axis=1, concat_axis=0, tiled=True),
        lax.all_to_all(values, "uly", split_axis=1, concat_axis=0, tiled=True),
    )
    query_rows, feature_width = q_part.shape
    head_count = feature_width // HEAD_DIM
    local_blocks = block_lists.shape[0]
    slot_count = block_lists.shape[1]
    total_blocks = lax.axis_size("blk") * local_blocks
    q_heads = q_part.reshape(query_rows, head_count, HEAD_DIM)
    score_scale = HEAD_DIM ** (-0.5)
    whole_keys, whole_values = (
        lax.all_gather(k_part, "blk", axis=0, tiled=True),
        lax.all_gather(v_part, "blk", axis=0, tiled=True),
    )
    key_table = whole_keys.reshape(total_blocks, BLOCK, head_count, HEAD_DIM)
    value_table = whole_values.reshape(total_blocks, BLOCK, head_count, HEAD_DIM)
    q_blocks = q_heads.reshape(local_blocks, BLOCK, head_count, HEAD_DIM)

    def attend_listed(operands):
        q_block, block_ids, used_count = operands
        key_sel = jnp.take(key_table, block_ids, axis=0)
        value_sel = jnp.take(value_table, block_ids, axis=0)
        scores = (
            jnp.einsum("qhd,skhd->hqsk", q_block, key_sel, preferred_element_type=jnp.float32)
            * score_scale
        )
        used = (jnp.arange(slot_count) < used_count)[None, None, :, None]
        scores = jnp.where(used, scores, -1e30)
        row_max = jnp.max(scores, axis=(2, 3))
        probs = jnp.where(used, jnp.exp(scores - row_max[:, :, None, None]), 0.0)
        denom = jnp.sum(probs, axis=(2, 3))
        mixed = jnp.einsum(
            "hqsk,skhd->qhd",
            probs.astype(jnp.bfloat16),
            value_sel,
            preferred_element_type=jnp.float32,
        )
        mixed = mixed / denom.T[:, :, None]
        return mixed.astype(jnp.bfloat16).reshape(BLOCK, head_count * HEAD_DIM)

    attended = lax.map(attend_listed, (q_blocks, block_lists, block_counts)).reshape(
        query_rows, feature_width
    )
    partial_value = jnp.dot(
        attended,
        lax.all_gather(out_weight, "blk", axis=1, tiled=True),
        preferred_element_type=jnp.float32,
    )
    summed = lax.psum_scatter(
        partial_value.astype(jnp.bfloat16), "uly", scatter_dimension=0, tiled=True
    ).astype(jnp.float32)
    return (out_gate * (summed + out_bias)).astype(jnp.bfloat16)


def solution(mesh):
    in_specs = (
        P(("blk", "uly"), None),
        P(("blk", "uly"), None),
        P(("blk", "uly"), None),
        P("blk", None),
        P("blk"),
        P("uly", "blk"),
        P(),
        P(),
    )
    out_specs = P(("blk", "uly"), None)
    return jax.shard_map(body, mesh=mesh, in_specs=in_specs, out_specs=out_specs, check_vma=False)
```

profile of v0, /device:TPU:70, one launch (start us, length us, event | category | flops | bytes accessed | tf_op | source)
XLA Modules:
  0.0 322.6 jit_solution(14820862387826043719)
XLA Ops:
  6.5 0.9 copy.74
  7.5 12.9 %all_to_all.54 = bf16[16,8,640]{2,0,1:T(8,128)(2,1)} all-to-all(bf16[16,8,640]{2,0,1:T(8,128)(2,1)S(1)} %bitcast.52), channel_id=1, replica_groups=mesh['blk'=32,'uly'=8] {'uly'}, dimensions={1} | all-to-all | bytes 327680 | tf_op jit(solution)/shard_map/all_to_all | solution.py:13
  20.5 0.9 copy.75
  21.4 11.4 %all_to_all.55 = bf16[16,8,640]{2,0,1:T(8,128)(2,1)} all-to-all(bf16[16,8,640]{2,0,1:T(8,128)(2,1)S(1)} %bitcast.53), channel_id=1, replica_groups=mesh['blk'=32,'uly'=8] {'uly'}, dimensions={1} | all-to-all | bytes 327680 | tf_op jit(solution)/shard_map/all_to_all | solution.py:14
  32.9 0.7 all-gather.8.cloned.1.call-update
  33.6 1.6 copy.73
  35.2 6.0 %all-to-all-start.2 = ((bf16[16,8,640]{2,0,1:T(8,128)(2,1)}), bf16[16,8,640]{2,0,1:T(8,128)(2,1)S(1)}, u32[]{:S(2)}, u32[]{:S(2)}) async-start(bf16[16,8,640]{2,0,1:T(8,128)(2,1)} %bitcast.45), calls=%async_computation.2 | async-start | bytes 327680 | tf_op jit(solution)/shard_map/all_to_all | solution.py:12
  42.5 0.7 compare_and_fusion
  43.2 3.6 %all-to-all-done.2 = bf16[16,8,640]{2,0,1:T(8,128)(2,1)S(1)} async-done(((bf16[16,8,640]{2,0,1:T(8,128)(2,1)}), bf16[16,8,640]{2,0,1:T(8,128)(2,1)S(1)}, u32[]{:S(2)}, u32[]{:S(2)}) %all-to-all-start.2) | async-done | bytes 163872 | tf_op jit(solution)/shard_map/all_to_all | solution.py:12
  47.0 41.4 %all-gather.6.cloned.1.call-done = bf16[4096,640]{1,0:T(8,128)(2,1)} async-done(((bf16[128,640]{1,0:T(8,128)(2,1)}), bf16[4096,640]{1,0:T(8,128)(2,1)}) %all-gather.6.cloned.1.call-update) | async-done | bytes 5242896 | tf_op jit(solution)/shard_map/all_gather | solution.py:24
  88.4 12.7 %reshape.65 = bf16[32,128,5,128]{3,2,1,0:T(8,128)(2,1)} reshape(bf16[4096,640]{1,0:T(8,128)(2,1)} %all-gather.6.cloned.1.call-done) | data formatting | bytes 10485760 | tf_op jit(solution)/shard_map/reshape | solution.py:27
  101.0 7.5 %copy.35 = bf16[32,128,5,128]{3,1,2,0:T(8,128)(2,1)} copy(bf16[32,128,5,128]{3,2,1,0:T(8,128)(2,1)} %reshape.65) | data formatting | bytes 10485760 | tf_op jit(solution)/shard_map/reshape | solution.py:27
  108.5 49.8 %all-gather.4.cloned.1.call-done = bf16[4096,640]{1,0:T(8,128)(2,1)} async-done(((bf16[128,640]{1,0:T(8,128)(2,1)}), bf16[4096,640]{1,0:T(8,128)(2,1)}) %all-gather.4.cloned.1.call-update) | async-done | bytes 5242896 | tf_op jit(solution)/shard_map/all_gather | solution.py:25
  158.3 12.7 %reshape.64 = bf16[32,128,5,128]{3,2,1,0:T(8,128)(2,1)} reshape(bf16[4096,640]{1,0:T(8,128)(2,1)} %all-gather.4.cloned.1.call-done) | data formatting | bytes 10485760 | tf_op jit(solution)/shard_map/reshape | solution.py:28
  170.9 7.4 %copy.32 = bf16[32,128,5,128]{3,1,2,0:T(8,128)(2,1)} copy(bf16[32,128,5,128]{3,2,1,0:T(8,128)(2,1)} %reshape.64) | data formatting | bytes 10485760 | tf_op jit(solution)/shard_map/reshape | solution.py:28
  178.4 4.7 %gather_fusion.1 = bf16[12,128,5,128]{3,1,2,0:T(8,128)(2,1)} fusion(bf16[32,128,5,128]{3,1,2,0:T(8,128)(2,1)} %copy.35, s32[1024]{0:T(1024)S(1)} %pad_clamp_fusion), kind=kCustom, calls=%fused_computation.1.clone | custom fusion | bytes 3932208 | tf_op jit(solution)/shard_map/while/body/eval_jaxpr/jit(_take)/gather | solution.py:33
  183.0 3.5 %gather_fusion = bf16[12,128,5,128]{3,1,2,0:T(8,128)(2,1)S(1)} fusion(bf16[32,128,5,128]{3,1,2,0:T(8,128)(2,1)} %copy.32, s32[1024]{0:T(1024)S(1)} %pad_clamp_fusion), kind=kCustom, calls=%fused_computation.clone | custom fusion | bytes 3932208 | tf_op jit(solution)/shard_map/while/body/eval_jaxpr/jit(_take)/gather | solution.py:34
  186.5 2.4 bitcast_reduce_fusion
  189.0 1.2 fusion.2
  190.2 0.9 fusion.20
  191.0 39.1 %all-gather.8.cloned.1.call-done = bf16[640,5120]{0,1:T(8,128)(2,1)} async-done(((bf16[640,160]{0,1:T(8,128)(2,1)}), bf16[640,5120]{0,1:T(8,128)(2,1)}) %all-gather.8.cloned.1.call-update) | async-done | bytes 6553616 | tf_op jit(solution)/shard_map/all_gather | solution.py:58
  230.1 6.2 %convolution_convert_fusion = bf16[128,5120]{1,0:T(8,128)(2,1)} fusion(bf16[128,640]{0,1:T(8,128)(2,1)S(1)} %bitcast.58, bf16[640,5120]{0,1:T(8,128)(2,1)} %all-gather.8.cloned.1.call-done), kind=kOutput, calls=%fused_computation.2 | convolution fusion | flops 839516160 | bytes 8028160 | tf_op jit(solution)/shard_map/dot_general | solution.py:56
  236.4 78.1 %reduce-scatter.2.cloned.1.call-done = bf16[16,5120]{1,0:T(8,128)(2,1)} async-done(((bf16[128,5120]{1,0:T(8,128)(2,1)}), bf16[16,5120]{1,0:T(8,128)(2,1)}) %reduce-scatter.2.cloned.1.call-update) | async-done | bytes 163856 | tf_op jit(solution)/shard_map/reduce_scatter | solution.py:61
  314.4 1.6 multiply_convert_fusion
  (15 shorter events, 1.0 us)
Async XLA Ops:
  6.5 81.8 %all-gather.6.cloned.1.call-start = ((), (), s32[]{:S(2)}) async-start(), calls=%async_computation.5 | async-start | bytes 5406720 | tf_op jit(solution)/shard_map/all_gather | solution.py:24
  20.4 137.9 %all-gather.4.cloned.1.call-start = ((), (), s32[]{:S(2)}) async-start(), calls=%async_computation.4 | async-start | bytes 5406720 | tf_op jit(solution)/shard_map/all_gather | solution.py:25
  32.8 197.3 %all-gather.8.cloned.1.call-start = ((), (), s32[]{:S(2)}) async-start(), calls=%async_computation.6 | async-start | bytes 6758400 | tf_op jit(solution)/shard_map/all_gather | solution.py:58
  35.2 11.6 %all-to-all-start.2 = ((bf16[16,8,640]{2,0,1:T(8,128)(2,1)}), bf16[16,8,640]{2,0,1:T(8,128)(2,1)S(1)}, u32[]{:S(2)}, u32[]{:S(2)}) async-start(bf16[16,8,640]{2,0,1:T(8,128)(2,1)} %bitcast.45), calls=%async_computation.2 | async-start | bytes 327680 | tf_op jit(solution)/shard_map/all_to_all | solution.py:12
  41.2 273.2 %reduce-scatter.2.cloned.1.call-start = ((), (), s32[]{:S(2)}) async-start(), calls=%async_computation.7 | async-start | bytes 1474560 | tf_op jit(solution)/shard_map/reduce_scatter | solution.py:61
  230.1 84.3 %copy-start = (f32[5120]{0:T(1024)S(1)}, f32[5120]{0:T(1024)}, u32[]{:S(2)}) copy-start(f32[5120]{0:T(1024)} %param.16) | copy-start | bytes 61444
  230.1 84.3 %copy-start.1 = (f32[5120]{0:T(1024)S(1)}, f32[5120]{0:T(1024)}, u32[]{:S(2)}) copy-start(f32[5120]{0:T(1024)} %param.17) | copy-start | bytes 61444
Sparse Core Ops, SparseCore 0:
  20.5 67.7 all-gather.5
  90.2 68.0 all-gather.3
  160.2 69.9 all-gather.7
  236.5 77.9 reduce-scatter.1
where the time goes:
time: 325 us; the launch traced here: 323 us
  waiting for transfers between devices  213 us (66%)
  local copies, waits for them, and re-layouts  52 us (16%)
  blocking collectives  24.3 us (7%)
  between operations  13.8 us (4%)
  matrix products  9.47 us (3%)
  starting transfers between devices  6.12 us (2%)
  other arithmetic  4.17 us (1%)
    reduce_scatter x1, waiting for transfers between devices, body(): lax.psum_scatter(partial_value.astype(jnp.bfloat16), 'uly', scatter_dimen...  78.1 us
    all_gather x1, waiting for transfers between devices, body(): lax.all_gather(v_part, 'blk', axis=0, tiled=True)  49.8 us
    all_gather x1, waiting for transfers between devices, body(): lax.all_gather(k_part, 'blk', axis=0, tiled=True)  41.4 us
    all_gather x1, waiting for transfers between devices, body(): lax.all_gather(out_weight, 'blk', axis=1, tiled=True)  39.1 us
    reshape x2, local copies, waits for them, and re-layouts, body(): key_table = whole_keys.reshape(total_blocks, BLOCK, head_count, HEAD_DIM)  20.1 us
    reshape x2, local copies, waits for them, and re-layouts, body(): whole_values.reshape(total_blocks, BLOCK, head_count, HEAD_DIM)  20.1 us
    all_to_all x1, blocking collectives, body(): lax.all_to_all(keys, 'uly', split_axis=1, concat_axis=0, tiled=True)  12.9 us
    all_to_all x1, blocking collectives, body(): lax.all_to_all(values, 'uly', split_axis=1, concat_axis=0, tiled=True)  11.4 us
  transfers between devices with their start and end apart: 5, of which 5 were waited for; matrix products, arithmetic and copies ran while one was open for 18% of the time, Pallas kernels for 0%

commit v1 on v0

v1 whole, which is shorter than its diff:
```python
import functools

import jax
import jax.numpy as jnp
from jax import lax
from jax.experimental import pallas as pl
from jax.experimental.pallas import tpu as pltpu
from jax.sharding import PartitionSpec as P

MESH = pl.DeviceIdType.MESH
HEAD_DIM = 128
SLOTS = 12
DZ = (0, 1, 7, 2, 6, 3, 5, 4)
BF16 = jnp.bfloat16
F32 = jnp.float32


def coords():
    b = lax.axis_index("blk")
    u = lax.axis_index("uly")
    return (u % 2) * 2 + (b // 2) % 2, u // 2, b // 4, b % 2


def dev(x, y, z, c):
    return (z * 4 + (x % 2) * 2 + c, y * 2 + x // 2)


def wait_bytes(ref, sem):
    pltpu.make_async_copy(ref, ref, sem).wait()


def remote(src, dst, send, recv, device):
    return pltpu.make_async_remote_copy(
        src, dst, send, recv, device_id=device, device_id_type=MESH
    )


def greet(devices):
    bar = pltpu.get_barrier_semaphore()
    for d in devices:
        pl.semaphore_signal(bar, inc=1, device_id=d, device_id_type=MESH)
    pl.semaphore_wait(bar, len(devices))


def w_step(s, wbuf, w_send, w_recv):
    x, y, z, c = coords()
    out = []
    for way, sign in ((0, 1), (1, -1)):
        zb = (z - sign * (s - 1) + 8) % 8
        part = wbuf.at[zb] if s < 4 else wbuf.at[zb, pl.ds(400 * way, 400)]
        out.append(
            remote(part, part, w_send.at[way, s - 1], w_recv.at[way, s - 1],
                   dev(x, y, (z + sign + 8) % 8, c))
        )
    return out


def w_start(s, *refs):
    for cp in w_step(s, *refs):
        cp.start()


def w_wait(s, wbuf, w_send, w_recv):
    z = coords()[2]
    for way, sign in ((0, 1), (1, -1)):
        zb = (z - sign * s + 8) % 8
        part = wbuf.at[zb] if s < 4 else wbuf.at[zb, pl.ds(400 * way, 400)]
        wait_bytes(part, w_recv.at[way, s - 1])


def gather_kernel(
    q_ref, k_ref, v_ref, w_ref, kv, qbuf, wbuf,
    stage, recv_a, recv_b,
    send_sem, a_sem, b_sem, kv_send, kv_sem, kvb_send, kvb_sem,
    sib_send, sib_sem, q_send, qb_send, q_sem, w_send, w_recv,
):
    x, y, z, c = coords()
    half = z // 4
    row = z % 4
    wrefs = (wbuf, w_send, w_recv)

    for h in range(40):
        cols = pl.ds(h * HEAD_DIM, HEAD_DIM)
        stage[h, 0] = k_ref[:, cols]
        stage[h, 1] = v_ref[:, cols]
        stage[h, 2] = q_ref[:, cols]

    peers = [
        dev(x, (y + dy) % 4, (z + dz) % 8, c)
        for dz in range(8) for dy in range(4) if (dy, dz) != (0, 0)
    ]
    peers += [
        dev((x + dx) % 4, y, half * 4 + (z + dr) % 4, c) for dr in range(4) for dx in (1, 2, 3)
    ]
    peers.append(dev(x, y, z, 1 - c))
    greet(peers)

    for dz in DZ:
        zd = (z + dz) % 8

        def send_a(dy, _, dz=dz, zd=zd):
            yd = (y + dy) % 4
            head = yd * 10 + (zd // 4) * 5 + zd % 4
            remote(stage.at[head], recv_a.at[z, y], send_sem, a_sem.at[dz],
                   dev(x, yd, zd, c)).start()
            return 0

        if dz == 0:
            head = y * 10 + half * 5 + row
            pltpu.make_async_copy(stage.at[head], recv_a.at[z, y], a_sem.at[0]).start()
        lax.fori_loop(1 if dz == 0 else 0, 4, send_a, 0)
    for dh in range(2):
        hd = (half + dh) % 2

        def send_b(dy, _, hd=hd):
            yd = (y + dy) % 4
            remote(stage.at[yd * 10 + hd * 5 + 4], recv_b.at[half, y], send_sem, b_sem.at[0],
                   dev(x, yd, hd * 4 + row, c)).start()
            return 0

        if dh == 0:
            pltpu.make_async_copy(
                stage.at[y * 10 + half * 5 + 4], recv_b.at[half, y], b_sem.at[0]
            ).start()
        lax.fori_loop(1 if dh == 0 else 0, 4, send_b, 0)

    wbuf[z, 0:640] = w_ref[:, 0:128]
    wbuf[z, 640:800] = jnp.concatenate(
        [w_ref[160 * g : 160 * g + 160, 128:160] for g in range(4)], axis=1
    )
    w_start(1, *wrefs)

    def forward(dz):
        zs = (z - dz + 8) % 8
        wait_bytes(recv_a.at[zs], a_sem.at[dz])
        src = recv_a.at[zs, :, pl.ds(0, 2)]
        dst = kv.at[x, c, zs // 4, zs % 4]
        for dx in range(4):
            xd = (x + dx) % 4

            @pl.when(xd < 3)
            def _(dx=dx, xd=xd):
                if dx == 0:
                    pltpu.make_async_copy(src, dst, kv_sem.at[dz]).start()
                else:
                    remote(src, dst, kv_send.at[dx - 1, dz], kv_sem.at[dz],
                           dev(xd, y, z, c)).start()

        part = zs // 3
        qsrc = recv_a.at[zs, :, 2]
        qdst = qbuf.at[x, zs % 3]

        @pl.when(part == x)
        def _():
            pltpu.make_async_copy(qsrc, qdst, q_sem.at[0]).start()

        @pl.when(part != x)
        def _():
            remote(qsrc, qdst, q_send.at[dz], q_sem.at[0], dev(part, y, z, c)).start()

    def to_sibling(dz):
        zs = (z - dz + 8) % 8

        @pl.when(x < 3)
        def _():
            got = kv.at[:, c, zs // 4, zs % 4]
            wait_bytes(got, kv_sem.at[dz])
            remote(got, got, sib_send.at[dz], sib_sem.at[dz], dev(x, y, z, 1 - c)).start()

    for i, dz in enumerate(DZ):
        forward(dz)
        if i >= 2:
            to_sibling(DZ[i - 2])
        if i == 3:
            w_wait(1, *wrefs)
            w_start(2, *wrefs)

    wait_bytes(recv_b, b_sem.at[0])
    bsrc = recv_b.at[:, :, pl.ds(0, 2)]
    bdst = kv.at[x, c, :, row]
    for dr in range(4):
        rd = (z + dr) % 4
        if dr == 0:
            @pl.when(x == 3)
            def _():
                pltpu.make_async_copy(bsrc, bdst, kvb_sem.at[0]).start()

            @pl.when(x != 3)
            def _():
                remote(bsrc, bdst, kvb_send.at[0], kvb_sem.at[0], dev(3, y, z, c)).start()
        else:
            remote(bsrc, bdst, kvb_send.at[dr], kvb_sem.at[dr],
                   dev(3, y, half * 4 + rd, c)).start()
    qsrc_b = recv_b.at[:, :, 2]
    qdst_b = qbuf.at[x, pl.ds(0, 2)]

    @pl.when(x == 3)
    def _():
        pltpu.make_async_copy(qsrc_b, qdst_b, q_sem.at[0]).start()

    @pl.when(x != 3)
    def _():
        remote(qsrc_b, qdst_b, qb_send.at[0], q_sem.at[0], dev(3, y, z, c)).start()

    to_sibling(DZ[6])
    w_wait(2, *wrefs)
    w_start(3, *wrefs)
    to_sibling(DZ[7])

    @pl.when(x == 3)
    def _():
        for dr in range(4):
            got = kv.at[:, c, :, (z - dr + 4) % 4]
            wait_bytes(got, kvb_sem.at[dr])
            remote(got, got, sib_send.at[dr], sib_sem.at[dr], dev(x, y, z, 1 - c)).start()

    @pl.when(x < 2)
    def _():
        wait_bytes(qbuf, q_sem.at[0])

    @pl.when(x >= 2)
    def _():
        wait_bytes(qbuf.at[:, pl.ds(0, 2)], q_sem.at[0])

    @pl.when(x < 3)
    def _():
        for dz in DZ:
            zs = (z - dz + 8) % 8
            wait_bytes(kv.at[:, 1 - c, zs // 4, zs % 4], sib_sem.at[dz])
            wait_bytes(kv.at[:, c, zs // 4, zs % 4], sib_send.at[dz])

    @pl.when(x == 3)
    def _():
        for dr in range(4):
            rs = (z - dr + 4) % 4
            wait_bytes(kv.at[:, 1 - c, :, rs], sib_sem.at[dr])
            wait_bytes(kv.at[:, c, :, rs], sib_send.at[dr])

    w_wait(3, *wrefs)
    w_start(4, *wrefs)
    wait_bytes(stage.at[pl.ds(0, 38)], send_sem)
    for dz in range(8):
        zs = (z - dz + 8) % 8
        for dx in (1, 2, 3):
            @pl.when((x + dx) % 4 < 3)
            def _(dx=dx):
                wait_bytes(recv_a.at[zs, :, pl.ds(0, 2)], kv_send.at[dx - 1, dz])

        @pl.when(zs // 3 != x)
        def _():
            wait_bytes(recv_a.at[zs, :, 2], q_send.at[dz])
    for dr in range(4):
        if dr == 0:
            @pl.when(x != 3)
            def _():
                wait_bytes(bsrc, kvb_send.at[0])
                wait_bytes(qsrc_b, qb_send.at[0])
        else:
            wait_bytes(bsrc, kvb_send.at[dr])
    w_wait(4, *wrefs)
    for s in (1, 2, 3, 4):
        for cp in w_step(s, *wrefs):
            cp.wait_send()


def attend_kernel(lists, kv, qbuf, att, kg, vg, sc, pr):
    x, y, z, c = coords()
    scale = float(HEAD_DIM ** -0.5 * 1.4426950408889634)

    def item(i, _):
        zi = i // 2
        xl = i % 2
        zq = jnp.where(x < 3, 3 * x + zi, zi * 4 + z % 4)
        blk = zq * 4 + xl * 2 + c
        count = lists[blk, SLOTS]
        q = jnp.concatenate(
            [qbuf[xl, zi].reshape(64, 128), qbuf[xl + 2, zi].reshape(64, 128)], axis=0
        )
        top = None
        for s in range(SLOTS):
            kb = lists[blk, s]
            kz = kb // 4
            for xh in range(2):
                got = kv.at[(kb // 2) % 2 + 2 * xh, kb % 2, kz // 4, kz % 4]
                rows = pl.ds(s * 128 + xh * 64, 64)
                kg[rows, :] = got[:, 0].reshape(64, 128)
                vg[rows, :] = got[:, 1].reshape(64, 128)
            part = lax.dot_general(
                q, kg[s * 128 : s * 128 + 128, :], (((1,), (1,)), ((), ())),
                preferred_element_type=F32,
            )
            part = jnp.where(s < count, part, -1e30)
            sc[s] = part
            top = part if top is None else jnp.maximum(top, part)
        top = jnp.max(top, axis=1, keepdims=True)
        den = jnp.zeros((128, 128), F32)
        for s in range(SLOTS):
            p = jnp.exp2((sc[s] - top) * scale)
            den = den + p
            pr[:, s * 128 : s * 128 + 128] = p.astype(BF16)
        mixed = jnp.dot(pr[...], vg[...], preferred_element_type=F32)
        den = jnp.sum(den, axis=1, keepdims=True)
        att[zi, xl] = (mixed / den).astype(BF16)
        return 0

    lax.fori_loop(0, jnp.where(x < 2, 6, 4), item, 0)


def project_kernel(
    att, wbuf, bias, gate, out,
    att_t, acat, wrest, psend, precv, rsum, rrecv,
    c_send, c_recv, s_send, s_recv, rs_send, rs_recv, f_send, f_recv,
):
    x, y, z, c = coords()
    half = z // 4
    xh = x // 2
    xl = x % 2
    peers = [
        dev((x + dx) % 4, y, (z + dz) % 8, c)
        for dz in range(8) for dx in range(4) if (dx, dz) != (0, 0)
    ]
    peers += [
        dev((x + 2 * dxh) % 4, (y + dy) % 4, z, c) for dy in (1, 2, 3) for dxh in range(2)
    ]
    other = xh * 2 + 1 - xl
    peers += [dev(x, y, z, 1 - c), dev(other, y, z, 1 - c)]
    greet(peers)

    j_mine = jnp.where(x < 3, z % 4, 4)

    def c_copies(act):
        for zi in range(3):
            zt = jnp.where(x < 3, 3 * x + zi, zi * 4 + z % 4) % 8
            for x2 in range(2):
                xd = half * 2 + x2
                here = (xd == x) & (zt == z)
                live = (x < 2) if zi == 2 else (x < 4)

                @pl.when(live & jnp.logical_not(here))
                def _(zi=zi, zt=zt, x2=x2, xd=xd):
                    act(zi, zt, x2, xd, False)

                @pl.when(live & here)
                def _(zi=zi, zt=zt, x2=x2, xd=xd):
                    act(zi, zt, x2, xd, True)

    def c_start(zi, zt, x2, xd, here):
        dst = att_t.at[j_mine, c]
        if here:
            pltpu.make_async_copy(att.at[zi], dst, c_recv.at[j_mine]).start()
        else:
            remote(att.at[zi], dst, c_send.at[zi, x2], c_recv.at[j_mine],
                   dev(xd, y, zt, c)).start()

    c_copies(c_start)

    for g in range(4):
        wrest[160 * g : 160 * g + 160, :] = jnp.concatenate(
            [wbuf[zz, 640:800, 32 * g : 32 * g + 32] for zz in range(8)], axis=1
        )

    for j in range(5):
        got = att_t.at[j, c]
        wait_bytes(got, c_recv.at[j])
        remote(got, got, s_send.at[j], s_recv.at[j], dev(x, y, z, 1 - c)).start()
    for j in range(5):
        wait_bytes(att_t.at[j, 1 - c], s_recv.at[j])
        for c2 in range(2):
            for x2 in range(2):
                r0 = (c2 * 2 + x2) * 128
                acat[r0 : r0 + 128, j * 128 : j * 128 + 128] = att_t[j, c2, x2]

    def rs_copy(n, dxh, dy):
        xd = (x + 2 * dxh) % 4
        yd = (y + dy) % 4
        return remote(psend.at[n, xd // 2 * 4 + yd], precv.at[n, xh * 4 + y],
                      rs_send.at[n], rs_recv.at[n], dev(xd, yd, z, c))

    order = [(1, 2), (0, 2), (1, 1), (1, 3), (1, 0), (0, 1), (0, 3)]
    for n in range(5):
        if n < 4:
            wn = jnp.concatenate([wbuf[2 * n, 0:640], wbuf[2 * n + 1, 0:640]], axis=1)
        else:
            wn = wrest[...]
        r = jnp.dot(acat[...], wn, preferred_element_type=F32).astype(BF16)
        for c2 in range(2):
            for x2 in range(2):
                r0 = (c2 * 2 + x2) * 128
                psend[n, :, c2, x2] = r[r0 : r0 + 128].reshape(8, 16, 256)
        for dxh, dy in order:
            rs_copy(n, dxh, dy).start()

    for n in range(5):
        wait_bytes(precv.at[n, pl.ds(0, 7)], rs_recv.at[n])
        mine = xh * 4 + y
        total = psend[n, mine].astype(F32)
        for d in range(1, 8):
            total = total + precv[n, (mine + d) % 8].astype(F32)
        rsum[:, :, n] = total.astype(BF16)

    finals = []
    for i, (dxl, dc) in enumerate(((1, 1), (1, 0), (0, 1))):
        xl2 = (xl + dxl) % 2
        c2 = (c + dc) % 2
        cp = remote(rsum.at[c2, xl2], rrecv.at[xl, c], f_send.at[i], f_recv.at[i],
                    dev(xh * 2 + xl2, y, z, c2))
        cp.start()
        finals.append(cp)
    rrecv[xl, c] = rsum[c, xl]
    for cp in finals:
        cp.wait_recv()

    lane = lax.broadcasted_iota(jnp.int32, (16, 128), 1)

    def glue(parts, shifts):
        out = None
        edge = 0
        for p, (shift, width) in zip(parts, shifts):
            moved = pltpu.roll(p, shift % 128, 1) if shift % 128 else p
            out = moved if out is None else jnp.where(lane >= edge, moved, out)
            edge += width
        return out

    for zz in range(8):
        m = []
        r = []
        for i in range(4):
            got = rrecv[i // 2, i % 2, zz // 2, :, (zz % 2) * 128 : (zz % 2) * 128 + 128]
            m.append(got.astype(F32))
            lo = (zz // 4) * 128
            got = rrecv[i // 2, i % 2, 4, :, lo : lo + 128].astype(F32)
            r.append(got)
        o = (32 * zz) % 128
        tiles = [
            m[0],
            glue([r[0], m[1]], [(-o, 32), (32, 96)]),
            glue([m[1], r[1], m[2]], [(32, 32), (32 - o, 32), (64, 64)]),
            glue([m[2], r[2], m[3]], [(64, 64), (64 - o, 32), (96, 32)]),
            glue([m[3], r[3]], [(96, 96), (96 - o, 32)]),
        ]
        for t in range(5):
            cols = slice(zz * 640 + t * 128, zz * 640 + t * 128 + 128)
            out[:, cols] = (gate[:, cols] * (tiles[t] + bias[:, cols])).astype(BF16)

    def c_done(zi, zt, x2, xd, here):
        if not here:
            wait_bytes(att.at[zi], c_send.at[zi, x2])

    c_copies(c_done)
    for j in range(5):
        wait_bytes(att_t.at[j, c], s_send.at[j])
    for n in range(5):
        wait_bytes(psend.at[n, pl.ds(0, 7)], rs_send.at[n])
    for cp in finals:
        cp.wait_send()


VM = pl.BlockSpec(memory_space=pltpu.VMEM)
SM = pl.BlockSpec(memory_space=pltpu.SMEM)
DMA = pltpu.SemaphoreType.DMA
LIMIT = 48 * 2**20


def body(queries, keys, values, block_lists, block_counts, out_weight, out_bias, out_gate):
    local = jnp.concatenate(
        [block_lists, block_counts[:, None], jnp.zeros((1, 3), jnp.int32)], axis=1
    )
    lists = lax.all_gather(local, "blk", axis=0, tiled=True)
    shape = jax.ShapeDtypeStruct
    kv, qbuf, wbuf = pl.pallas_call(
        gather_kernel,
        out_shape=(
            shape((4, 2, 2, 4, 4, 2, 16, 128), BF16),
            shape((4, 3, 4, 16, 128), BF16),
            shape((8, 800, 128), BF16),
        ),
        in_specs=[VM] * 4,
        out_specs=(VM, VM, VM),
        scratch_shapes=[
            pltpu.VMEM((40, 3, 16, 128), BF16),
            pltpu.VMEM((8, 4, 3, 16, 128), BF16),
            pltpu.VMEM((2, 4, 3, 16, 128), BF16),
            DMA, DMA((8,)), DMA((1,)), DMA((3, 8)), DMA((8,)), DMA((4,)), DMA((4,)),
            DMA((8,)), DMA((8,)), DMA((8,)), DMA((1,)), DMA((1,)), DMA((2, 4)), DMA((2, 4)),
        ],
        compiler_params=pltpu.CompilerParams(
            collective_id=0, has_side_effects=True, vmem_limit_bytes=LIMIT
        ),
        name="gather",
    )(queries, keys, values, out_weight)
    att = pl.pallas_call(
        attend_kernel,
        out_shape=shape((3, 2, 128, 128), BF16),
        in_specs=[SM, VM, VM],
        out_specs=VM,
        scratch_shapes=[
            pltpu.VMEM((SLOTS * 128, 128), BF16),
            pltpu.VMEM((SLOTS * 128, 128), BF16),
            pltpu.VMEM((SLOTS, 128, 128), F32),
            pltpu.VMEM((128, SLOTS * 128), BF16),
        ],
        compiler_params=pltpu.CompilerParams(vmem_limit_bytes=LIMIT),
        name="attend",
    )(lists, kv, qbuf)
    return pl.pallas_call(
        project_kernel,
        out_shape=shape((16, 5120), BF16),
        in_specs=[VM] * 4,
        out_specs=VM,
        scratch_shapes=[
            pltpu.VMEM((5, 2, 2, 128, 128), BF16),
            pltpu.VMEM((512, 640), BF16),
            pltpu.VMEM((640, 256), BF16),
            pltpu.VMEM((5, 8, 2, 2, 16, 256), BF16),
            pltpu.VMEM((5, 8, 2, 2, 16, 256), BF16),
            pltpu.VMEM((2, 2, 5, 16, 256), BF16),
            pltpu.VMEM((2, 2, 5, 16, 256), BF16),
            DMA((3, 2)), DMA((5,)), DMA((5,)), DMA((5,)), DMA((5,)), DMA((5,)),
            DMA((3,)), DMA((3,)),
        ],
        compiler_params=pltpu.CompilerParams(
            collective_id=1, has_side_effects=True, vmem_limit_bytes=LIMIT
        ),
        name="project",
    )(att, wbuf, out_bias.reshape(1, -1), out_gate.reshape(1, -1))


def solution(mesh):
    in_specs = (
        P(("blk", "uly"), None),
        P(("blk", "uly"), None),
        P(("blk", "uly"), None),
        P("blk", None),
        P("blk"),
        P("uly", "blk"),
        P(),
        P(),
    )
    out_specs = P(("blk", "uly"), None)
    return jax.shard_map(body, mesh=mesh, in_specs=in_specs, out_specs=out_specs, check_vma=False)
```

time: 325 us -> 147 us (0.45)
  the two profiles are of different devices: /device:TPU:70 before, /device:TPU:64 now
where the time goes in v1:
time: 147 us
  Pallas kernels  114 us (78%)
  blocking collectives  26.9 us (18%)
  local copies, waits for them, and re-layouts  4.53 us (3%)
    pallas_call x1, Pallas kernels, body(): pl.pallas_call(project_kernel, out_shape=shape((16, 5120), BF16), in_spec...  59.1 us
    pallas_call x1, Pallas kernels, body(): pl.pallas_call(gather_kernel, out_shape=(shape((4, 2, 2, 4, 4, 2, 16, 128...  48.8 us
    all_gather x1, blocking collectives, body(): lists = lax.all_gather(local, 'blk', axis=0, tiled=True)  26.9 us
    pallas_call x1, Pallas kernels, body(): pl.pallas_call(attend_kernel, out_shape=shape((3, 2, 128, 128), BF16), in...  6.08 us
    unnamed x12, local copies, waits for them, and re-layouts  4.53 us

profile of v1, /device:TPU:64, one launch (start us, length us, event | category | flops | bytes accessed | tf_op | source)
XLA Modules:
  0.0 146.8 jit_solution(1611553086681778356)
XLA Ops:
  0.0 0.0 copy-start.3
  0.0 0.0 copy-start.4
  0.0 1.1 copy.11.w_ref
  1.1 0.0 copy-start
  1.1 0.9 copy-done
  2.0 0.0 copy-start.1
  2.0 0.9 copy-done.1
  3.0 0.0 copy-start.2
  3.0 0.9 copy-done.2
  3.9 48.8 %gather.1 = (bf16[4,2,2,4,4,2,16,128]{7,6,5,4,3,2,1,0:T(8,128)(2,1)S(1)}, bf16[4,3,4,16,128]{4,3,2,1,0:T(8,128)(2,1)S(1)}, bf16[8,800,128]{2,1,0:T(8,128)(2,1)S(1)}) custom-call(bf16[16,5120]{1,0:T(8,128)(2,1)S(1)} %copy-done, bf16[16,5120]{1,0:T(8,128)(2,1)S(1)} %copy-done.1, bf16[16,5120]{1,0:T(8,128)(2,1)S(1)} %copy-done.2, bf16[640,160]{1,0:T(8,128)(2,1)S(1)} %copy.11.w_ref), custom_call_target="tpu_custom_call" | custom-call | tf_op jit(solution)/shard_map/gather/pallas_call | solution.py:470
  53.3 0.7 fusion
  54.1 26.9 %all-gather = s32[32,1,16]{2,1,0:T(1,128)S(1)} all-gather(s32[1,1,16]{2,1,0:T(1,128)S(1)} %fusion), channel_id=1, replica_groups=mesh['blk'=32,'uly'=8] {'blk'}, dimensions={0}, use_global_device_ids=true | all-gather | bytes 2112 | tf_op jit(solution)/shard_map/all_gather | solution.py:468
  80.9 6.1 %attend.1.att = bf16[3,2,128,128]{3,2,1,0:T(8,128)(2,1)S(1)} custom-call(s32[32,16]{1,0:T(8,128)S(1)} %bitcast.11, bf16[4,2,2,4,4,2,16,128]{7,6,5,4,3,2,1,0:T(8,128)(2,1)S(1)} %get-tuple-element.8.kv, bf16[4,3,4,16,128]{4,3,2,1,0:T(8,128)(2,1)S(1)} %get-tuple-element.9.qbuf), custom_call_target="tpu_custom_call" | custom-call | tf_op jit(solution)/shard_map/attend/pallas_call | solution.py:491
  87.0 0.0 copy-done.3
  87.0 0.0 copy-done.4
  87.0 59.1 %project.1 = bf16[16,5120]{1,0:T(8,128)(2,1)S(1)} custom-call(bf16[3,2,128,128]{3,2,1,0:T(8,128)(2,1)S(1)} %attend.1.att, bf16[8,800,128]{2,1,0:T(8,128)(2,1)S(1)} %get-tuple-element.10.wbuf, f32[1,5120]{1,0:T(1,128)S(1)} %bitcast.12, f32[1,5120]{1,0:T(1,128)S(1)} %bitcast.13), custom_call_target="tpu_custom_call" | custom-call | tf_op jit(solution)/shard_map/project/pallas_call | solution.py:505
  146.1 0.7 copy.14
  (1 shorter events, 0.0 us)
Async XLA Ops:
  0.0 87.0 %copy-start.3 = (f32[5120]{0:T(1024)S(1)}, f32[5120]{0:T(1024)}, u32[]{:S(2)}) copy-start(f32[5120]{0:T(1024)} %param.14) | copy-start | bytes 61444
  0.0 87.0 %copy-start.4 = (f32[5120]{0:T(1024)S(1)}, f32[5120]{0:T(1024)}, u32[]{:S(2)}) copy-start(f32[5120]{0:T(1024)} %param.15) | copy-start | bytes 61444
  1.1 0.9 copy-start
  2.0 0.9 copy-start.1
  3.0 0.9 copy-start.2

commit v2 on v0

v2 whole, which is shorter than its diff:
```python
import functools

import jax
import jax.numpy as jnp
from jax import lax
from jax.experimental import pallas as pl
from jax.experimental.pallas import tpu as pltpu
from jax.sharding import PartitionSpec as P

MESH = pl.DeviceIdType.MESH
HEAD_DIM = 128
SLOTS = 12
DZ = (0, 1, 7, 2, 6, 3, 5, 4)
BF16 = jnp.bfloat16
F32 = jnp.float32


def coords():
    b = lax.axis_index("blk")
    u = lax.axis_index("uly")
    return (u % 2) * 2 + (b // 2) % 2, u // 2, b // 4, b % 2


def dev(x, y, z, c):
    return (z * 4 + (x % 2) * 2 + c, y * 2 + x // 2)


def wait_bytes(ref, sem):
    pltpu.make_async_copy(ref, ref, sem).wait()


def remote(src, dst, send, recv, device):
    return pltpu.make_async_remote_copy(
        src, dst, send, recv, device_id=device, device_id_type=MESH
    )


def mega_kernel(
    q_ref, k_ref, v_ref, lists_ref, counts_ref, w_ref, bias, gate, out,
    stage, recv_a, recv_b, kv, qbuf, lbuf, lsm, kg, vg, sc, pr, att, att_t,
    wsrc, wbuf, acat, wrest, psend, precv, rsum, rrecv,
    send_sem, a_sem, b_sem, kv_send, kv_sem, kvb_send, kvb_sem,
    sib_send, sib_sem, q_send, qb_send, q_sem, l_send, l_recv, l_sem,
    wx_send, wx_recv, w_send, w_recv, ws_send, ws_recv,
    c_send, c_recv, r_send, r_recv, rs_send, rs_recv, f_send, f_recv,
):
    x, y, z, c = coords()
    half = z // 4
    row = z % 4
    xh = x // 2
    xl = x % 2

    for h in range(40):
        cols = pl.ds(h * HEAD_DIM, HEAD_DIM)
        stage[h, 0] = k_ref[:, cols]
        stage[h, 1] = v_ref[:, cols]
        stage[h, 2] = q_ref[:, cols]
    lbuf[xl, z] = jnp.full((1, 128), counts_ref[0], jnp.int32)
    lbuf[xl, z, :, 0:SLOTS] = lists_ref[...]

    peers = [
        dev(x, (y + dy) % 4, (z + dz) % 8, c)
        for dz in range(8) for dy in range(4) if (dy, dz) != (0, 0)
    ]
    peers += [dev((x + dx) % 4, y, (z + dz) % 8, c) for dz in range(8) for dx in (1, 2, 3)]
    peers += [dev(x, y, z, 1 - c), dev((x + 2) % 4, y, z, 1 - c)]
    bar = pltpu.get_barrier_semaphore()
    for d in peers:
        pl.semaphore_signal(bar, inc=1, device_id=d, device_id_type=MESH)
    wsrc[0:640] = w_ref[:, 0:128]
    wsrc[640:800] = jnp.concatenate(
        [w_ref[160 * g : 160 * g + 160, 128:160] for g in range(4)], axis=1
    )
    pl.semaphore_wait(bar, len(peers))

    for dz in range(1, 8):
        remote(lbuf.at[xl, z], lbuf.at[xl, z], l_send.at[dz], l_recv.at[dz],
               dev(x, y, (z + dz) % 8, c)).start()

    def stage1_a(dz):
        zd = (z + dz) % 8

        def send_a(dy, _):
            yd = (y + dy) % 4
            head = yd * 10 + (zd // 4) * 5 + zd % 4
            remote(stage.at[head], recv_a.at[z, y], send_sem, a_sem.at[dz],
                   dev(x, yd, zd, c)).start()
            return 0

        if dz == 0:
            head = y * 10 + half * 5 + row
            pltpu.make_async_copy(stage.at[head], recv_a.at[z, y], a_sem.at[0]).start()
        lax.fori_loop(1 if dz == 0 else 0, 4, send_a, 0)

    def stage1_b():
        for dh in range(2):
            hd = (half + dh) % 2

            def send_b(dy, _, hd=hd):
                yd = (y + dy) % 4
                remote(stage.at[yd * 10 + hd * 5 + 4], recv_b.at[half, y], send_sem,
                       b_sem.at[0], dev(x, yd, hd * 4 + row, c)).start()
                return 0

            if dh == 0:
                pltpu.make_async_copy(
                    stage.at[y * 10 + half * 5 + 4], recv_b.at[half, y], b_sem.at[0]
                ).start()
            lax.fori_loop(1 if dh == 0 else 0, 4, send_b, 0)

    for dz in DZ[:B_AT]:
        stage1_a(dz)
    stage1_b()
    for dz in DZ[B_AT:]:
        stage1_a(dz)

    @pl.when(xh == c)
    def _():
        pltpu.make_async_copy(wsrc, wbuf.at[c, z], wx_recv.at[0]).start()

    @pl.when(xh != c)
    def _():
        remote(wsrc, wbuf.at[xh, z], wx_send.at[0], wx_recv.at[0],
               dev((x + 2) % 4, y, z, 1 - c)).start()

    def w_part(zb, s, way):
        return wbuf.at[c, zb] if s < 4 else wbuf.at[c, zb, pl.ds(400 * way, 400)]

    def w_copies(s):
        got = []
        for way, sign in ((0, 1), (1, -1)):
            part = w_part((z - sign * (s - 1) + 8) % 8, s, way)
            got.append(remote(part, part, w_send.at[way, s - 1], w_recv.at[way, s - 1],
                              dev(x, y, (z + sign + 8) % 8, c)))
        return got

    def w_sib(zb, k):
        part = wbuf.at[c, zb]
        return remote(part, part, ws_send.at[k], ws_recv.at[k], dev(x, y, z, 1 - c))

    def w_start(s):
        if s == 1:
            wait_bytes(wbuf.at[c, z], wx_recv.at[0])
        else:
            for way, sign in ((0, 1), (1, -1)):
                part = w_part((z - sign * (s - 1) + 8) % 8, s - 1, way)
                wait_bytes(part, w_recv.at[way, s - 2])
        if s < 5:
            for cp in w_copies(s):
                cp.start()
        if s == 1:
            w_sib(z, 0).start()
        elif s < 5:
            w_sib((z - s + 9) % 8, 2 * s - 3).start()
            w_sib((z + s - 1) % 8, 2 * s - 2).start()
        else:
            w_sib((z + 4) % 8, 7).start()

    def w_order():
        got = [(0, z)]
        for s in (2, 3, 4):
            got += [(2 * s - 3, (z - s + 9) % 8), (2 * s - 2, (z + s - 1) % 8)]
        return got + [(7, (z + 4) % 8)]

    def forward(dz):
        zs = (z - dz + 8) % 8
        wait_bytes(recv_a.at[zs], a_sem.at[dz])
        src = recv_a.at[zs, :, pl.ds(0, 2)]
        dst = kv.at[x, c, zs // 4, zs % 4]
        for dx in (2, 1, 3, 0):
            xd = (x + dx) % 4

            @pl.when(xd < 3)
            def _(dx=dx, xd=xd):
                if dx == 0:
                    pltpu.make_async_copy(src, dst, kv_sem.at[dz]).start()
                else:
                    remote(src, dst, kv_send.at[dx - 1, dz], kv_sem.at[dz],
                           dev(xd, y, z, c)).start()

        part = zs // 3
        qsrc = recv_a.at[zs, :, 2]
        qdst = qbuf.at[x, zs % 3]

        @pl.when(part == x)
        def _():
            pltpu.make_async_copy(qsrc, qdst, q_sem.at[0]).start()

        @pl.when(part != x)
        def _():
            remote(qsrc, qdst, q_send.at[dz], q_sem.at[0], dev(part, y, z, c)).start()

    def to_sibling(dz):
        zs = (z - dz + 8) % 8

        @pl.when(x < 3)
        def _():
            got = kv.at[:, c, zs // 4, zs % 4]
            wait_bytes(got, kv_sem.at[dz])
            remote(got, got, sib_send.at[dz], sib_sem.at[dz], dev(x, y, z, 1 - c)).start()

    bsrc = recv_b.at[:, :, pl.ds(0, 2)]
    bdst = kv.at[x, c, :, row]
    qsrc_b = recv_b.at[:, :, 2]
    qdst_b = qbuf.at[x, pl.ds(0, 2)]

    def forward_b():
        wait_bytes(recv_b, b_sem.at[0])
        for dr in (2, 1, 3, 0):
            rd = (z + dr) % 4
            if dr == 0:
                @pl.when(x == 3)
                def _():
                    pltpu.make_async_copy(bsrc, bdst, kvb_sem.at[0]).start()
                    pltpu.make_async_copy(qsrc_b, qdst_b, q_sem.at[0]).start()

                @pl.when(x != 3)
                def _():
                    remote(bsrc, bdst, kvb_send.at[0], kvb_sem.at[0], dev(3, y, z, c)).start()
                    remote(qsrc_b, qdst_b, qb_send.at[0], q_sem.at[0], dev(3, y, z, c)).start()
            else:
                remote(bsrc, bdst, kvb_send.at[dr], kvb_sem.at[dr],
                       dev(3, y, half * 4 + rd, c)).start()

    def forward_lists():
        for dz in range(1, 8):
            wait_bytes(lbuf.at[xl, (z - dz + 8) % 8], l_recv.at[dz])
        remote(lbuf.at[xl], lbuf.at[xl], l_send.at[0], l_recv.at[0],
               dev(xh * 2 + 1 - xl, y, z, c)).start()

    def place_lists():
        wait_bytes(lbuf.at[1 - xl], l_recv.at[0])
        cp = pltpu.make_async_copy(lbuf, lsm, l_sem.at[0])
        cp.start()
        cp.wait()

    for i, dz in enumerate(DZ):
        forward(dz)
        if i >= 2:
            to_sibling(DZ[i - 2])
        if i == B_FWD:
            forward_b()
        if i == W1_AT:
            w_start(1)
        if i == W2_AT:
            w_start(2)
    forward_lists()
    to_sibling(DZ[6])
    to_sibling(DZ[7])

    @pl.when(x == 3)
    def _():
        for dr in range(4):
            got = kv.at[:, c, :, (z - dr + 4) % 4]
            wait_bytes(got, kvb_sem.at[dr])
            remote(got, got, sib_send.at[dr], sib_sem.at[dr], dev(x, y, z, 1 - c)).start()

    place_lists()

    @pl.when(x < 2)
    def _():
        wait_bytes(qbuf, q_sem.at[0])

    @pl.when(x >= 2)
    def _():
        wait_bytes(qbuf.at[:, pl.ds(0, 2)], q_sem.at[0])

    @pl.when(x < 3)
    def _():
        for dz in DZ:
            zs = (z - dz + 8) % 8
            wait_bytes(kv.at[:, 1 - c, zs // 4, zs % 4], sib_sem.at[dz])

    @pl.when(x == 3)
    def _():
        for dr in range(4):
            wait_bytes(kv.at[:, 1 - c, :, (z - dr + 4) % 4], sib_sem.at[dr])

    if W2_AT >= 8:
        w_start(2)

    scale = float(HEAD_DIM ** -0.5 * 1.4426950408889634)
    j_mine = jnp.where(x < 3, row, 4)
    h_mine = half * 5 + j_mine
    slot_mine = jnp.where(x < 3, half, 2)
    n_zi = jnp.where(x < 2, 3, 2)

    def c_place(zi, l):
        zt = jnp.where(x < 3, 3 * x + zi, zi * 4 + row) % 8
        xd = jnp.where(x < 3, row, half * 2 + l)
        return zt, xd, (zt == z) & (xd == x)

    def item(zi, l):
        zq = jnp.where(x < 3, 3 * x + zi, zi * 4 + row) % 8
        count = lsm[l, zq, 0, SLOTS]
        q = jnp.concatenate(
            [qbuf[l, zi].reshape(64, 128), qbuf[l + 2, zi].reshape(64, 128)], axis=0
        )
        top = None
        for s in range(SLOTS):
            kb = lsm[l, zq, 0, s]
            kz = kb // 4
            for a in range(2):
                rows = pl.ds(s * 128 + a * 64, 64)
                got = kv[(kb // 2) % 2 + 2 * a, kb % 2, kz // 4, kz % 4]
                kg[rows, :] = got[:, 0].reshape(64, 128)
                vg[rows, :] = got[:, 1].reshape(64, 128)
            part = lax.dot_general(
                q, kg[s * 128 : s * 128 + 128, :], (((1,), (1,)), ((), ())),
                preferred_element_type=F32,
            )
            part = jnp.where(s < count, part, -1e30)
            sc[s] = part
            top = part if top is None else jnp.maximum(top, part)
        top = jnp.max(top, axis=1, keepdims=True)
        den = jnp.zeros((128, 128), F32)
        for s in range(SLOTS):
            p = jnp.exp2((sc[s] - top) * scale)
            den = den + p
            pr[:, s * 128 : s * 128 + 128] = p.astype(BF16)
        mixed = jnp.dot(pr[...], vg[...], preferred_element_type=F32)
        den = jnp.sum(den, axis=1, keepdims=True)
        att[zi, l] = (mixed / den).astype(BF16)
        zt, xd, here = c_place(zi, l)
        src = att.at[zi, l]
        dst = att_t.at[l, h_mine]
        sem = c_recv.at[l, slot_mine]

        @pl.when(here)
        def _():
            pltpu.make_async_copy(src, dst, sem).start()

        @pl.when(jnp.logical_not(here))
        def _():
            remote(src, dst, c_send.at[l, zi], sem, dev(xd, y, zt, c)).start()

    def items(l):
        def step(zi, _):
            item(zi, l)
            return 0

        lax.fori_loop(0, n_zi, step, 0)

    def relay_one(l, h, k):
        got = att_t.at[l, h]
        wait_bytes(got, c_recv.at[l, k])
        for dx in (2, 1, 3):
            remote(got, got, r_send.at[l, k, dx - 1], r_recv.at[l, h],
                   dev((x + dx) % 4, y, z, c)).start()

    def relay(l):
        relay_one(l, x, 0)
        relay_one(l, 5 + x, 1)

        @pl.when(xl == l)
        def _():
            relay_one(l, xh * 5 + 4, 2)

    def relayed(l):
        for h in range(10):
            source = h % 5 if h % 5 < 4 else (h // 5) * 2 + l

            @pl.when(x != source)
            def _(h=h):
                wait_bytes(att_t.at[l, h], r_recv.at[l, h])

            acat[:, h * 128 : h * 128 + 128] = att_t[l, h]

    def rs_copy(l, g, dy):
        yd = (y + dy) % 4
        cols = pl.ds(0, 3) if g == 0 else pl.ds(3, 2)
        return remote(psend.at[l, yd, cols], precv.at[l, y, cols], rs_send.at[l, g, dy - 1],
                      rs_recv.at[l, g], dev(x, yd, z, c))

    def project(l):
        for n in range(5):
            if n < 4:
                wn = [
                    jnp.concatenate([wbuf[k, 2 * n, 0:640], wbuf[k, 2 * n + 1, 0:640]], axis=1)
                    for k in range(2)
                ]
            else:
                wn = [wrest[0], wrest[1]]
            r = jnp.dot(acat[:, 0:640], wn[0], preferred_element_type=F32)
            r = r + jnp.dot(acat[:, 640:1280], wn[1], preferred_element_type=F32)
            r = r.astype(BF16).reshape(2, 4, 16, 256)
            for yy in range(4):
                for a in range(2):
                    psend[l, yy, n, a] = r[a, yy]
            if n in (2, 4):
                for dy in (2, 1, 3):
                    rs_copy(l, n // 4, dy).start()

    def f_place(l, a):
        return a * 2 + l

    def reduce(l):
        for g in range(2):
            cols = slice(0, 3) if g == 0 else slice(3, 5)
            wait_bytes(precv.at[l, pl.ds(0, 3), pl.ds(0, 3) if g == 0 else pl.ds(3, 2)],
                       rs_recv.at[l, g])
            total = psend[l, y, cols].astype(F32)
            for d in (1, 2, 3):
                total = total + precv[l, (y + d) % 4, cols].astype(F32)
            total = total.astype(BF16)
            for a in range(2):
                rsum[l, a, cols] = total[:, a]
        for a in range(2):
            xd = f_place(l, a)

            @pl.when(xd == x)
            def _(a=a):
                rrecv[x] = rsum[l, a]

            @pl.when(xd != x)
            def _(a=a, xd=xd):
                remote(rsum.at[l, a], rrecv.at[x], f_send.at[l, a], f_recv.at[x],
                       dev(xd, y, z, c)).start()

    items(0)
    w_start(3)
    items(1)
    relay(0)
    w_start(4)
    relay(1)
    w_start(5)
    for k, zb in w_order():
        wait_bytes(wbuf.at[1 - c, zb], ws_recv.at[k])
    for k in range(2):
        for g in range(4):
            wrest[k, 160 * g : 160 * g + 160, :] = jnp.concatenate(
                [wbuf[k, zz, 640:800, 32 * g : 32 * g + 32] for zz in range(8)], axis=1
            )
    relayed(0)
    project(0)
    relayed(1)
    project(1)
    reduce(0)
    reduce(1)

    for d in (1, 2, 3):
        xs = (x + d) % 4
        wait_bytes(rrecv.at[xs], f_recv.at[xs])
    lane = lax.broadcasted_iota(jnp.int32, (16, 128), 1)

    def glue(parts, shifts):
        made = None
        edge = 0
        for p, (shift, width) in zip(parts, shifts):
            moved = pltpu.roll(p, shift % 128, 1) if shift % 128 else p
            made = moved if made is None else jnp.where(lane >= edge, moved, made)
            edge += width
        return made

    for zz in range(8):
        m = []
        r = []
        lo = (zz // 4) * 128
        for i in range(4):
            xs = (i % 2) * 2 + i // 2
            got = rrecv[xs, zz // 2, :, (zz % 2) * 128 : (zz % 2) * 128 + 128]
            m.append(got.astype(F32))
            r.append(rrecv[xs, 4, :, lo : lo + 128].astype(F32))
        o = (32 * zz) % 128
        tiles = [
            m[0],
            glue([r[0], m[1]], [(-o, 32), (32, 96)]),
            glue([m[1], r[1], m[2]], [(32, 32), (32 - o, 32), (64, 64)]),
            glue([m[2], r[2], m[3]], [(64, 64), (64 - o, 32), (96, 32)]),
            glue([m[3], r[3]], [(96, 96), (96 - o, 32)]),
        ]
        for t in range(5):
            cols = slice(zz * 640 + t * 128, zz * 640 + t * 128 + 128)
            out[:, cols] = (gate[:, cols] * (tiles[t] + bias[:, cols])).astype(BF16)

    wait_bytes(stage.at[pl.ds(0, 38)], send_sem)
    for dz in range(1, 8):
        wait_bytes(lbuf.at[xl, z], l_send.at[dz])
    wait_bytes(lbuf.at[xl], l_send.at[0])

    @pl.when(xh != c)
    def _():
        wait_bytes(wsrc, wx_send.at[0])

    for dz in range(8):
        zs = (z - dz + 8) % 8
        for dx in (1, 2, 3):
            @pl.when((x + dx) % 4 < 3)
            def _(dx=dx):
                wait_bytes(recv_a.at[zs, :, pl.ds(0, 2)], kv_send.at[dx - 1, dz])

        @pl.when(zs // 3 != x)
        def _():
            wait_bytes(recv_a.at[zs, :, 2], q_send.at[dz])
    for dr in range(4):
        if dr == 0:
            @pl.when(x != 3)
            def _():
                wait_bytes(bsrc, kvb_send.at[0])
                wait_bytes(qsrc_b, qb_send.at[0])
        else:
            wait_bytes(bsrc, kvb_send.at[dr])

    @pl.when(x < 3)
    def _():
        for dz in DZ:
            zs = (z - dz + 8) % 8
            wait_bytes(kv.at[:, c, zs // 4, zs % 4], sib_send.at[dz])

    @pl.when(x == 3)
    def _():
        for dr in range(4):
            wait_bytes(kv.at[:, c, :, (z - dr + 4) % 4], sib_send.at[dr])

    for s in (1, 2, 3, 4):
        for cp in w_copies(s):
            cp.wait_send()
    for k, zb in w_order():
        wait_bytes(wbuf.at[c, zb], ws_send.at[k])
    for l in range(2):
        for zi in range(3):
            zt, xd, here = c_place(zi, l)

            @pl.when((zi < n_zi) & jnp.logical_not(here))
            def _(l=l, zi=zi):
                wait_bytes(att.at[zi, l], c_send.at[l, zi])
        for dx in (1, 2, 3):
            wait_bytes(att_t.at[l, x], r_send.at[l, 0, dx - 1])
            wait_bytes(att_t.at[l, 5 + x], r_send.at[l, 1, dx - 1])

            @pl.when(xl == l)
            def _(l=l, dx=dx):
                wait_bytes(att_t.at[l, xh * 5 + 4], r_send.at[l, 2, dx - 1])
        for g in range(2):
            for dy in (1, 2, 3):
                rs_copy(l, g, dy).wait_send()
        for a in range(2):
            @pl.when(f_place(l, a) != x)
            def _(l=l, a=a):
                wait_bytes(rsum.at[l, a], f_send.at[l, a])


VM = pl.BlockSpec(memory_space=pltpu.VMEM)
SM = pl.BlockSpec(memory_space=pltpu.SMEM)
DMA = pltpu.SemaphoreType.DMA
LIMIT = 48 * 2**20
B_AT = 3
B_FWD = 5
W1_AT = 2
W2_AT = 8


def body(queries, keys, values, block_lists, block_counts, out_weight, out_bias, out_gate):
    vm = pltpu.VMEM
    return pl.pallas_call(
        mega_kernel,
        out_shape=jax.ShapeDtypeStruct((16, 5120), BF16),
        in_specs=[VM, VM, VM, VM, SM, VM, VM, VM],
        out_specs=VM,
        scratch_shapes=[
            vm((40, 3, 16, 128), BF16),
            vm((8, 4, 3, 16, 128), BF16),
            vm((2, 4, 3, 16, 128), BF16),
            vm((4, 2, 2, 4, 4, 2, 16, 128), BF16),
            vm((4, 3, 4, 16, 128), BF16),
            vm((2, 8, 1, 128), jnp.int32),
            pltpu.SMEM((2, 8, 1, 128), jnp.int32),
            vm((SLOTS * 128, 128), BF16),
            vm((SLOTS * 128, 128), BF16),
            vm((SLOTS, 128, 128), F32),
            vm((128, SLOTS * 128), BF16),
            vm((3, 2, 128, 128), BF16),
            vm((2, 10, 128, 128), BF16),
            vm((800, 128), BF16),
            vm((2, 8, 800, 128), BF16),
            vm((128, 1280), BF16),
            vm((2, 640, 256), BF16),
            vm((2, 4, 5, 2, 16, 256), BF16),
            vm((2, 4, 5, 2, 16, 256), BF16),
            vm((2, 2, 5, 16, 256), BF16),
            vm((4, 5, 16, 256), BF16),
            DMA, DMA((8,)), DMA((1,)), DMA((3, 8)), DMA((8,)), DMA((4,)), DMA((4,)),
            DMA((8,)), DMA((8,)), DMA((8,)), DMA((1,)), DMA((1,)), DMA((8,)), DMA((8,)), DMA((1,)),
            DMA((1,)), DMA((1,)), DMA((2, 4)), DMA((2, 4)), DMA((8,)), DMA((8,)),
            DMA((2, 3)), DMA((2, 3)), DMA((2, 3, 3)), DMA((2, 10)), DMA((2, 2, 3)), DMA((2, 2)),
            DMA((2, 2)), DMA((4,)),
        ],
        compiler_params=pltpu.CompilerParams(
            collective_id=0, has_side_effects=True, vmem_limit_bytes=LIMIT
        ),
        name="block_sparse_attention",
    )(queries, keys, values, block_lists, block_counts, out_weight,
      out_bias.reshape(1, -1), out_gate.reshape(1, -1))


def solution(mesh):
    in_specs = (
        P(("blk", "uly"), None),
        P(("blk", "uly"), None),
        P(("blk", "uly"), None),
        P("blk", None),
        P("blk"),
        P("uly", "blk"),
        P(),
        P(),
    )
    out_specs = P(("blk", "uly"), None)
    return jax.shard_map(body, mesh=mesh, in_specs=in_specs, out_specs=out_specs, check_vma=False)
```

time: 325 us -> 81.7 us (0.25)
  waiting for transfers between devices: 213 us -> 0 us
  Pallas kernels: 0 us -> 77.5 us
  local copies, waits for them, and re-layouts: 52 us -> 1.86 us
  blocking collectives: 24.3 us -> 0 us
  between operations: 13.8 us -> 0.77 us
  matrix products: 9.47 us -> 0 us
  starting transfers between devices: 6.12 us -> 0 us
  other arithmetic: 4.17 us -> 0 us
    all_gather x3 -> x0, waiting for transfers between devices: 130 us -> none  [the longest x1 49.8 us: body(): lax.all_gather(v_part, 'blk', axis=0, tiled=True)]
    reduce_scatter x1 -> x0, waiting for transfers between devices: 78.1 us -> none  [body(): lax.psum_scatter(partial_value.astype(jnp.bfloat16), 'uly', scatter_dimen...]
    pallas_call x0 -> x1, Pallas kernels: none -> 77.5 us  [body(): pl.pallas_call(mega_kernel, out_shape=jax.ShapeDtypeStruct((16, 5120), BF...]
    reshape x4 -> x0, local copies, waits for them, and re-layouts: 40.2 us -> none  [the longest x2 20.1 us: body(): key_table = whole_keys.reshape(total_blocks, BLOCK, head_count, HEAD_DIM)]
    all_to_all x2 -> x0, blocking collectives: 24.3 us -> none  [the longest x1 12.9 us: body(): lax.all_to_all(keys, 'uly', split_axis=1, concat_axis=0, tiled=True)]
    dot_general x3 -> x0, matrix products: 9.47 us -> none  [the longest x1 6.19 us: body(): jnp.dot(attended, lax.all_gather(out_weight, 'blk', axis=1, tiled=True),...]
    gather x2 -> x0, local copies, waits for them, and re-layouts: 8.15 us -> none  [the longest x1 4.65 us: attend_listed(): key_sel = jnp.take(key_table, block_ids, axis=0)]
    all_to_all x1 -> x0, starting transfers between devices: 6.03 us -> none  [body(): lax.all_to_all(queries, 'uly', split_axis=1, concat_axis=0, tiled=True)]
  transfers between devices with their start and end apart: 5 -> 0, of which waited for: 5 -> 0; matrix products, arithmetic and copies ran while one was open for 18% -> 0% of each run, Pallas kernels for 0% -> 0%
where the time goes in v2:
time: 81.7 us; the launch traced here: 80.2 us
  Pallas kernels  77.5 us (95%)
  local copies, waits for them, and re-layouts  1.86 us (2%)
    pallas_call x1, Pallas kernels, body(): pl.pallas_call(mega_kernel, out_shape=jax.ShapeDtypeStruct((16, 5120), BF...  77.5 us
    unnamed x14, local copies, waits for them, and re-layouts  1.86 us

profile of v2, /device:TPU:70, one launch (start us, length us, event | category | flops | bytes accessed | tf_op | source)
XLA Modules:
  0.0 80.2 jit_solution(10042121380933582062)
XLA Ops:
  0.0 0.0 copy-start.5
  0.7 0.0 copy-start
  0.7 0.0 copy-start.1
  0.7 0.0 copy-start.2
  0.7 0.0 copy-start.3
  0.7 0.0 copy-start.4
  0.7 1.2 %copy.9.w_ref = bf16[640,160]{1,0:T(8,128)(2,1)S(1)} copy(bf16[640,160]{0,1:T(8,128)(2,1)} %param.13) | data formatting | bytes 409600 | tf_op args[5]
  1.9 0.0 copy-done.5
  1.9 0.0 copy-done
  1.9 0.0 copy-done.1
  1.9 0.0 copy-done.2
  1.9 0.0 copy-done.3
  1.9 0.0 copy-done.4
  1.9 77.5 %block_sparse_attention.1 = bf16[16,5120]{1,0:T(8,128)(2,1)S(1)} custom-call(bf16[16,5120]{1,0:T(8,128)(2,1)S(1)} %copy-done, bf16[16,5120]{1,0:T(8,128)(2,1)S(1)} %copy-done.1, bf16[16,5120]{1,0:T(8,128)(2,1)S(1)} %copy-done.2, s32[1,12]{1,0:T(1,128)S(1)} %copy-done.5, s32[1]{0:T(128)S(6)} %copy.11.counts_ref, bf16[640,160]{1,0:T(8,128)(2,1)S(1)} %copy.9.w_ref, ...), custom_call_target="tpu_custom_call" | custom-call | tf_op jit(solution)/shard_map/block_sparse_attention/pallas_call | solution.py:555
  79.5 0.7 copy.12
Async XLA Ops:
  0.0 1.9 %copy-start.5 = (s32[1,12]{1,0:T(1,128)S(1)}, s32[1,12]{1,0:T(1,128)}, u32[]{:S(2)}) copy-start(s32[1,12]{1,0:T(1,128)} %lists_ref.1) | copy-start | bytes 148
  0.7 1.2 %copy-start = (bf16[16,5120]{1,0:T(8,128)(2,1)S(1)}, bf16[16,5120]{1,0:T(8,128)(2,1)}, u32[]{:S(2)}) copy-start(bf16[16,5120]{1,0:T(8,128)(2,1)} %q_ref.1) | copy-start | bytes 491524
  0.7 1.2 %copy-start.1 = (bf16[16,5120]{1,0:T(8,128)(2,1)S(1)}, bf16[16,5120]{1,0:T(8,128)(2,1)}, u32[]{:S(2)}) copy-start(bf16[16,5120]{1,0:T(8,128)(2,1)} %k_ref.1) | copy-start | bytes 491524
  0.7 1.2 %copy-start.2 = (bf16[16,5120]{1,0:T(8,128)(2,1)S(1)}, bf16[16,5120]{1,0:T(8,128)(2,1)}, u32[]{:S(2)}) copy-start(bf16[16,5120]{1,0:T(8,128)(2,1)} %v_ref.1) | copy-start | bytes 491524
  0.7 1.2 %copy-start.3 = (f32[5120]{0:T(1024)S(1)}, f32[5120]{0:T(1024)}, u32[]{:S(2)}) copy-start(f32[5120]{0:T(1024)} %param.14) | copy-start | bytes 61444
  0.7 1.2 %copy-start.4 = (f32[5120]{0:T(1024)S(1)}, f32[5120]{0:T(1024)}, u32[]{:S(2)}) copy-start(f32[5120]{0:T(1024)} %param.15) | copy-start | bytes 61444

commit v3 on v0

v3 whole, which is shorter than its diff:
```python
import functools

import jax
import jax.numpy as jnp
from jax import lax
from jax.experimental import pallas as pl
from jax.experimental.pallas import tpu as pltpu
from jax.sharding import PartitionSpec as P

MESH = pl.DeviceIdType.MESH
HEAD_DIM = 128
SLOTS = 12
FEWEST = 4
DZ = (0, 1, 7, 2, 6, 3, 5, 4)
BF16 = jnp.bfloat16
F32 = jnp.float32


def coords():
    b = lax.axis_index("blk")
    u = lax.axis_index("uly")
    return (u % 2) * 2 + (b // 2) % 2, u // 2, b // 4, b % 2


def dev(x, y, z, c):
    return (z * 4 + (x % 2) * 2 + c, y * 2 + x // 2)


def wait_bytes(ref, sem):
    pltpu.make_async_copy(ref, ref, sem).wait()


def remote(src, dst, send, recv, device):
    return pltpu.make_async_remote_copy(
        src, dst, send, recv, device_id=device, device_id_type=MESH
    )


def mega_kernel(
    q_ref, k_ref, v_ref, lists_ref, counts_ref, w_ref, bias, gate, out,
    lin, bin_, gin, recv_a, recv_b, recv_q, kv, qbuf, lbuf, lsm,
    sc, att, att_t, wbuf, acat, psend, precv, rsum, rrecv,
    a_send, b_send, a_sem, b_sem, kv_send, kv_sem,
    sib_send, sib_sem, q_send, q_sem, l_send, l_recv, l_sem,
    wx_send, wx_recv, w_send, w_recv, ws_send, ws_recv,
    c_send, c_recv, r_send, r_recv, rs_send, rs_recv, f_send, f_recv, in_sem,
):
    x, y, z, c = coords()
    half = z // 4
    row = z % 4
    xh = x // 2
    xl = x % 2
    double = row == y
    z_base = jnp.where(double, 4 * (x % 2), 2 * x)
    n_zi = jnp.where(double, 4, 2)
    j_mine = jnp.where(double & (x >= 2), 4, row)

    peers = [
        dev(x, (y + dy) % 4, (z + dz) % 8, c)
        for dz in range(8) for dy in range(4) if (dy, dz) != (0, 0)
    ]
    peers += [dev((x + dx) % 4, y, (z + dz) % 8, c) for dz in range(8) for dx in (1, 2, 3)]
    peers += [dev(x, y, z, 1 - c), dev((x + 2) % 4, y, z, 1 - c)]
    bar = pltpu.get_barrier_semaphore()
    for d in peers:
        pl.semaphore_signal(bar, inc=1, device_id=d, device_id_type=MESH)
    loads = [
        pltpu.make_async_copy(src, dst, in_sem.at[i])
        for i, (src, dst) in enumerate(((lists_ref, lin), (bias, bin_), (gate, gin)))
    ]
    for cp in loads:
        cp.start()
    loads[0].wait()
    lbuf[xl, z] = jnp.full((1, 128), counts_ref[0], jnp.int32)
    lbuf[xl, z, :, 0:SLOTS] = lin[...]
    pl.semaphore_wait(bar, len(peers))

    ruler = kv.reshape(512, 16, 128)

    def wait_blocks(n, sem):
        wait_bytes(ruler.at[pl.ds(0, n)], sem)

    def lists_z():
        for dz in range(1, 8):
            remote(lbuf.at[xl, z], lbuf.at[xl, z], l_send.at[dz], l_recv.at[dz],
                   dev(x, y, (z + dz) % 8, c)).start()

    def stage1(dz):
        zd = (z + dz) % 8
        hd = zd // 4
        rd = zd % 4

        def go(head, yd, here, *refs):
            dst, dst_q, send, recv = refs
            cols = pl.ds(pl.multiple_of(head * HEAD_DIM, HEAD_DIM), HEAD_DIM)
            for src, to in ((k_ref, dst.at[z, y, 0]), (v_ref, dst.at[z, y, 1]), (q_ref, dst_q)):
                if here:
                    pltpu.make_async_copy(src.at[:, cols], to, recv).start()
                else:
                    remote(src.at[:, cols], to, send, recv, dev(x, yd, zd, c)).start()

        def loop(dy, _, here=False):
            yd = (y + dy) % 4
            go(yd * 10 + hd * 5 + rd, yd, here, recv_a, recv_q.at[0, z, y], a_send, a_sem.at[dz])
            return 0

        if dz == 0:
            loop(0, 0, True)
        lax.fori_loop(1 if dz == 0 else 0, 4, loop, 0)
        fifth = functools.partial(go, rd * 10 + hd * 5 + 4, rd)
        refs = (recv_b, recv_q.at[1, z, y], b_send, b_sem.at[dz])
        if dz == 0:
            @pl.when(double)
            def _():
                fifth(True, *refs)

            @pl.when(jnp.logical_not(double))
            def _():
                fifth(False, *refs)
        else:
            fifth(False, *refs)

    slot = (0, 2, 4, 6, 7, 5, 3, 1)

    def w_exchange():
        @pl.when(xh == c)
        def _():
            pltpu.make_async_copy(w_ref, wbuf.at[c, 0], wx_recv.at[0]).start()

        @pl.when(xh != c)
        def _():
            remote(w_ref, wbuf.at[xh, 0], wx_send.at[0], wx_recv.at[0],
                   dev((x + 2) % 4, y, z, 1 - c)).start()

    def w_part(d, s, way):
        at = wbuf.at[c, slot[d % 8]]
        return at if s < 4 else at.at[pl.ds(80 * way, 80)]

    def w_copies(s):
        got = []
        for way, sign in ((0, 1), (1, -1)):
            got.append(remote(
                w_part(-sign * (s - 1), s, way), w_part(-sign * s, s, way),
                w_send.at[way, s - 1], w_recv.at[way, s - 1],
                dev(x, y, (z + sign + 8) % 8, c),
            ))
        return got

    def w_sib(d):
        at = wbuf.at[c, slot[d]]
        return remote(at, at, ws_send.at[d], ws_recv.at[d], dev(x, y, z, 1 - c))

    def w_start(s):
        if s == 1:
            wait_bytes(wbuf.at[c, 0], wx_recv.at[0])
        else:
            for way, sign in ((0, 1), (1, -1)):
                wait_bytes(w_part(-sign * (s - 1), s - 1, way), w_recv.at[way, s - 2])
        if s < 5:
            for cp in w_copies(s):
                cp.start()
        for d in {1: (0,), 2: (7, 1), 3: (6, 2), 4: (5, 3), 5: (4,)}[s]:
            w_sib(d).start()

    def forward(dz):
        zs = (z - dz + 8) % 8
        wait_blocks(12, a_sem.at[dz])

        @pl.when(double)
        def _():
            wait_blocks(12, b_sem.at[dz])

        dst = kv.at[x, c, zs]
        for dx in (2, 1, 3, 0):
            xd = (x + dx) % 4
            second = double & (xd >= 2)
            for take, src in ((jnp.logical_not(second), recv_a), (second, recv_b)):
                src = src.at[zs]

                @pl.when(take)
                def _(dx=dx, xd=xd, src=src):
                    if dx == 0:
                        pltpu.make_async_copy(src, dst, kv_sem.at[dz]).start()
                    else:
                        remote(src, dst, kv_send.at[dx - 1, dz], kv_sem.at[dz],
                               dev(xd, y, z, c)).start()

        xq = jnp.where(double, zs // 4, zs // 2)
        dst_q = qbuf.at[x, jnp.where(double, zs % 4, zs % 2)]

        def go(src, xd, k):
            @pl.when(xd == x)
            def _():
                pltpu.make_async_copy(src, dst_q, q_sem.at[0]).start()

            @pl.when(xd != x)
            def _():
                remote(src, dst_q, q_send.at[k, dz], q_sem.at[0], dev(xd, y, z, c)).start()

        go(recv_q.at[0, zs], xq, 0)

        @pl.when(double)
        def _():
            go(recv_q.at[1, zs], 2 + zs // 4, 1)

    def to_sibling(dz):
        got = kv.at[:, c, (z - dz + 8) % 8]
        wait_bytes(got, kv_sem.at[dz])
        remote(got, got, sib_send.at[dz], sib_sem.at[dz], dev(x, y, z, 1 - c)).start()

    def forward_lists():
        for dz in range(1, 8):
            wait_bytes(lbuf.at[xl, (z - dz + 8) % 8], l_recv.at[dz])
        remote(lbuf.at[xl], lbuf.at[xl], l_send.at[0], l_recv.at[0],
               dev(xh * 2 + 1 - xl, y, z, c)).start()

    def place_lists():
        wait_bytes(lbuf.at[1 - xl], l_recv.at[0])
        cp = pltpu.make_async_copy(lbuf, lsm, l_sem.at[0])
        cp.start()
        cp.wait()

    act = {
        "S": stage1, "F": forward, "T": to_sibling, "W": w_start,
        "X": w_exchange, "L": lists_z, "l": forward_lists,
    }
    for step in SEQ:
        act[step[0]](*[int(n) for n in step[1:]])

    place_lists()

    @pl.when(double)
    def _():
        wait_bytes(qbuf, q_sem.at[0])

    @pl.when(jnp.logical_not(double))
    def _():
        wait_bytes(qbuf.at[:, pl.ds(0, 2)], q_sem.at[0])

    for dz in DZ:
        wait_bytes(kv.at[:, 1 - c, (z - dz + 8) % 8], sib_sem.at[dz])

    scale = float(HEAD_DIM ** -0.5 * 1.4426950408889634)
    h_mine = half * 5 + j_mine
    slot_mine = jnp.where(j_mine < 4, half, 2)

    def c_place(zi, l):
        zt = (z_base + zi) % 8
        xd = jnp.where(j_mine < 4, row, half * 2 + l)
        return zt, xd, (zt == z) & (xd == x)

    def item_scores(zi, l, n):
        zq = (z_base + zi) % 8
        count = lsm[l, zq, 0, SLOTS]
        q = jnp.concatenate(
            [qbuf[l, zi].reshape(64, 128), qbuf[l + 2, zi].reshape(64, 128)], axis=0
        )
        blocks = [lsm[l, zq, 0, s] for s in range(SLOTS)]
        top = None
        for s in range(SLOTS):
            part = lax.dot_general(
                q, rows_of(blocks[s], 0), (((1,), (1,)), ((), ())), preferred_element_type=F32
            )
            if s >= FEWEST:
                part = jnp.where(s < count, part, -1e30)
            sc[n, s] = part
            top = part if top is None else jnp.maximum(top, part)
        return blocks, jnp.max(top, axis=1, keepdims=True)

    def item_values(zi, l, n, blocks, top):
        den = jnp.zeros((128, 128), F32)
        mixed = jnp.zeros((128, 128), F32)
        for s in range(0, SLOTS, 2):
            pair = []
            for t in (s, s + 1):
                p = jnp.exp2((sc[n, t] - top) * scale)
                den = den + p
                pair.append(p.astype(BF16))
            mixed = mixed + jnp.dot(
                jnp.concatenate(pair, axis=1),
                jnp.concatenate([rows_of(blocks[s], 1), rows_of(blocks[s + 1], 1)], axis=0),
                preferred_element_type=F32,
            )
        den = jnp.sum(den, axis=1, keepdims=True)
        att[zi, l] = (mixed / den).astype(BF16)

    def rows_of(kb, which):
        return jnp.concatenate(
            [kv[(kb // 2) % 2 + 2 * a, kb % 2, kb // 4, :, which].reshape(64, 128) for a in range(2)],
            axis=0,
        )

    def item_send(zi, l):
        zt, xd, here = c_place(zi, l)
        src = att.at[zi, l]
        dst = att_t.at[l, h_mine]
        sem = c_recv.at[l, slot_mine]

        @pl.when(here)
        def _():
            pltpu.make_async_copy(src, dst, sem).start()

        @pl.when(jnp.logical_not(here))
        def _():
            remote(src, dst, c_send.at[l, zi], sem, dev(xd, y, zt, c)).start()

    def items(l):
        def step(i, _):
            first = item_scores(2 * i, l, 0)
            second = item_scores(2 * i + 1, l, 1)
            item_values(2 * i, l, 0, *first)
            item_values(2 * i + 1, l, 1, *second)
            item_send(2 * i, l)
            item_send(2 * i + 1, l)
            return 0

        lax.fori_loop(0, n_zi // 2, step, 0)

    def relay_one(l, h, k):
        got = att_t.at[l, h]
        wait_bytes(got, c_recv.at[l, k])
        for dx in (2, 1, 3):
            remote(got, got, r_send.at[l, k, dx - 1], r_recv.at[l, h],
                   dev((x + dx) % 4, y, z, c)).start()

    def relay(l, k):
        if k < 2:
            relay_one(l, 5 * k + x, k)
        else:
            @pl.when(xl == l)
            def _():
                relay_one(l, xh * 5 + 4, 2)

    def relayed(l):
        for h in range(10):
            source = h % 5 if h % 5 < 4 else (h // 5) * 2 + l

            @pl.when(x != source)
            def _(h=h):
                wait_bytes(att_t.at[l, h], r_recv.at[l, h])

            acat[l, :, h * 128 : h * 128 + 128] = att_t[l, h]

    def rs_copy(l, t, dy):
        yd = (y + dy) % 4
        return remote(psend.at[l, yd, t], precv.at[l, y, t], rs_send.at[l, t, dy - 1],
                      rs_recv.at[l, t], dev(x, yd, z, c))

    def from_sibling(s):
        for d in {1: (0,), 2: (7, 1), 3: (6, 2), 4: (5, 3), 5: (4,)}[s]:
            wait_bytes(wbuf.at[1 - c, slot[d]], ws_recv.at[d])

    def project(l, t):
        r = None
        for k in range(2):
            w = wbuf.reshape(2, 1280, 640)[k, 256 * t : 256 * t + 256]
            got = lax.dot_general(
                acat[l, :, 640 * k : 640 * k + 640], w, (((1,), (1,)), ((), ())),
                preferred_element_type=F32,
            )
            r = got if r is None else r + got
        r = r.astype(BF16).reshape(2, 4, 16, 256)
        for yy in range(4):
            for a in range(2):
                psend[l, yy, t, a] = r[a, yy]
        for dy in (2, 1, 3):
            rs_copy(l, t, dy).start()

    def f_place(l, a):
        return a * 2 + l

    def reduce(l):
        for t in (0, 1, 2, 3, 4):
            wait_bytes(precv.at[l, pl.ds(0, 3), t], rs_recv.at[l, t])
            total = psend[l, y, t].astype(F32)
            for d in (1, 2, 3):
                total = total + precv[l, (y + d) % 4, t].astype(F32)
            total = total.astype(BF16)
            for a in range(2):
                rsum[l, a, t] = total[a]
        for a in range(2):
            xd = f_place(l, a)

            @pl.when(xd == x)
            def _(a=a):
                rrecv[x] = rsum[l, a]

            @pl.when(xd != x)
            def _(a=a, xd=xd):
                remote(rsum.at[l, a], rrecv.at[x], f_send.at[l, a], f_recv.at[x],
                       dev(xd, y, z, c)).start()

    act = {
        "I": items, "R": relay, "G": relayed, "P": project, "D": reduce, "W": w_start,
        "V": from_sibling,
    }
    for step in SEQ_OUT:
        act[step[0]](*[int(n) for n in step[1:]])

    for d in (1, 2, 3):
        xs = (x + d) % 4
        wait_bytes(rrecv.at[xs], f_recv.at[xs])
    loads[1].wait()
    loads[2].wait()
    quarters = [
        jnp.concatenate([rrecv[xs, t].astype(F32) for t in range(5)], axis=1) for xs in (0, 2, 1, 3)
    ]
    for d in range(8):
        lo = 160 * slot[d]
        made = jnp.concatenate([part[:, lo : lo + 160] for part in quarters], axis=1)
        cols = pl.ds(pl.multiple_of((z + d) % 8 * 640, 128), 640)
        out[:, cols] = (gin[:, cols] * (made + bin_[:, cols])).astype(BF16)

    wait_blocks(31 * 3, a_send)
    for take, n in ((double, 7), (jnp.logical_not(double), 8)):
        @pl.when(take)
        def _(n=n):
            wait_blocks(n * 3, b_send)
    for dz in range(1, 8):
        wait_bytes(lbuf.at[xl, z], l_send.at[dz])
    wait_bytes(lbuf.at[xl], l_send.at[0])

    @pl.when(xh != c)
    def _():
        wait_bytes(w_ref, wx_send.at[0])

    for dz in range(8):
        zs = (z - dz + 8) % 8
        for dx in (1, 2, 3):
            wait_bytes(kv.at[x, c, zs], kv_send.at[dx - 1, dz])
        xq = jnp.where(double, zs // 4, zs // 2)

        @pl.when(xq != x)
        def _():
            wait_bytes(recv_q.at[0, zs], q_send.at[0, dz])

        @pl.when(double & (2 + zs // 4 != x))
        def _():
            wait_bytes(recv_q.at[1, zs], q_send.at[1, dz])

        wait_bytes(kv.at[:, c, zs], sib_send.at[dz])

    for s in (1, 2, 3, 4):
        for cp in w_copies(s):
            cp.wait_send()
    for d in range(8):
        w_sib(d).wait_send()
    for l in range(2):
        for zi in range(4):
            zt, xd, here = c_place(zi, l)

            @pl.when((zi < n_zi) & jnp.logical_not(here))
            def _(l=l, zi=zi):
                wait_bytes(att.at[zi, l], c_send.at[l, zi])
        for dx in (1, 2, 3):
            wait_bytes(att_t.at[l, x], r_send.at[l, 0, dx - 1])
            wait_bytes(att_t.at[l, 5 + x], r_send.at[l, 1, dx - 1])

            @pl.when(xl == l)
            def _(l=l, dx=dx):
                wait_bytes(att_t.at[l, xh * 5 + 4], r_send.at[l, 2, dx - 1])
        for t in range(5):
            for dy in (1, 2, 3):
                rs_copy(l, t, dy).wait_send()
        for a in range(2):
            @pl.when(f_place(l, a) != x)
            def _(l=l, a=a):
                wait_bytes(rsum.at[l, a], f_send.at[l, a])


VM = pl.BlockSpec(memory_space=pltpu.VMEM)
SM = pl.BlockSpec(memory_space=pltpu.SMEM)
DMA = pltpu.SemaphoreType.DMA
LIMIT = 63 * 2**20
HBM = pl.BlockSpec(memory_space=pl.ANY)
SEQ = (
    "X", "L", "S0", "S1", "S7", "S2", "S6", "S3", "S5", "S4", "F0", "F1", "F7", "T0", "W1", "F2",
    "F6", "T1", "T7", "F3", "F5", "T2", "T6", "F4", "W2", "l", "T3", "T5", "T4",
)
SEQ_OUT = (
    "I0", "W3", "I1", "R00", "R01", "R02", "W4", "R10", "R11", "R12", "G0", "V1", "V2", "V3",
    "P00", "P01", "P02", "V4", "P03", "W5", "V5", "P04", "G1", "P10", "P11", "P12", "P13", "P14",
    "D0", "D1",
)


def body(queries, keys, values, block_lists, block_counts, out_weight, out_bias, out_gate):
    vm = pltpu.VMEM
    return pl.pallas_call(
        mega_kernel,
        out_shape=jax.ShapeDtypeStruct((16, 5120), BF16),
        in_specs=[HBM, HBM, HBM, HBM, SM, HBM, HBM, HBM],
        out_specs=VM,
        scratch_shapes=[
            vm((1, SLOTS), jnp.int32),
            vm((1, 5120), F32),
            vm((1, 5120), F32),
            vm((8, 4, 2, 16, 128), BF16),
            vm((8, 4, 2, 16, 128), BF16),
            vm((2, 8, 4, 16, 128), BF16),
            vm((4, 2, 8, 4, 2, 16, 128), BF16),
            vm((4, 4, 4, 16, 128), BF16),
            vm((2, 8, 1, 128), jnp.int32),
            pltpu.SMEM((2, 8, 1, 128), jnp.int32),
            vm((2, SLOTS, 128, 128), F32),
            vm((4, 2, 128, 128), BF16),
            vm((2, 10, 128, 128), BF16),
            vm((2, 8, 160, 640), BF16),
            vm((2, 128, 1280), BF16),
            vm((2, 4, 5, 2, 16, 256), BF16),
            vm((2, 4, 5, 2, 16, 256), BF16),
            vm((2, 2, 5, 16, 256), BF16),
            vm((4, 5, 16, 256), BF16),
            DMA, DMA, DMA((8,)), DMA((8,)), DMA((3, 8)), DMA((8,)),
            DMA((8,)), DMA((8,)), DMA((2, 8)), DMA((1,)), DMA((8,)), DMA((8,)), DMA((1,)),
            DMA((1,)), DMA((1,)), DMA((2, 4)), DMA((2, 4)), DMA((8,)), DMA((8,)),
            DMA((2, 4)), DMA((2, 3)), DMA((2, 3, 3)), DMA((2, 10)), DMA((2, 5, 3)), DMA((2, 5)),
            DMA((2, 2)), DMA((4,)), DMA((3,)),
        ],
        compiler_params=pltpu.CompilerParams(
            collective_id=0, has_side_effects=True, vmem_limit_bytes=LIMIT
        ),
        name="block_sparse_attention",
    )(queries, keys, values, block_lists, block_counts, out_weight.T,
      out_bias.reshape(1, -1), out_gate.reshape(1, -1))


def solution(mesh):
    in_specs = (
        P(("blk", "uly"), None),
        P(("blk", "uly"), None),
        P(("blk", "uly"), None),
        P("blk", None),
        P("blk"),
        P("uly", "blk"),
        P(),
        P(),
    )
    out_specs = P(("blk", "uly"), None)
    return jax.shard_map(body, mesh=mesh, in_specs=in_specs, out_specs=out_specs, check_vma=False)
```

time: 325 us -> 69.9 us (0.22)
  waiting for transfers between devices: 213 us -> 0 us
  Pallas kernels: 0 us -> 67.5 us
  local copies, waits for them, and re-layouts: 52 us -> 1.59 us
  blocking collectives: 24.3 us -> 0 us
  between operations: 13.8 us -> 0.66 us
  matrix products: 9.47 us -> 0 us
  starting transfers between devices: 6.12 us -> 0 us
  other arithmetic: 4.17 us -> 0 us
    all_gather x3 -> x0, waiting for transfers between devices: 130 us -> none  [the longest x1 49.8 us: body(): lax.all_gather(v_part, 'blk', axis=0, tiled=True)]
    reduce_scatter x1 -> x0, waiting for transfers between devices: 78.1 us -> none  [body(): lax.psum_scatter(partial_value.astype(jnp.bfloat16), 'uly', scatter_dimen...]
    pallas_call x0 -> x1, Pallas kernels: none -> 67.5 us  [body(): pl.pallas_call(mega_kernel, out_shape=jax.ShapeDtypeStruct((16, 5120), BF...]
    reshape x4 -> x0, local copies, waits for them, and re-layouts: 40.2 us -> none  [the longest x2 20.1 us: body(): key_table = whole_keys.reshape(total_blocks, BLOCK, head_count, HEAD_DIM)]
    all_to_all x2 -> x0, blocking collectives: 24.3 us -> none  [the longest x1 12.9 us: body(): lax.all_to_all(keys, 'uly', split_axis=1, concat_axis=0, tiled=True)]
    dot_general x3 -> x0, matrix products: 9.47 us -> none  [the longest x1 6.19 us: body(): jnp.dot(attended, lax.all_gather(out_weight, 'blk', axis=1, tiled=True),...]
    gather x2 -> x0, local copies, waits for them, and re-layouts: 8.15 us -> none  [the longest x1 4.65 us: attend_listed(): key_sel = jnp.take(key_table, block_ids, axis=0)]
    all_to_all x1 -> x0, starting transfers between devices: 6.03 us -> none  [body(): lax.all_to_all(queries, 'uly', split_axis=1, concat_axis=0, tiled=True)]
  transfers between devices with their start and end apart: 5 -> 0, of which waited for: 5 -> 0; matrix products, arithmetic and copies ran while one was open for 18% -> 0% of each run, Pallas kernels for 0% -> 0%
where the time goes in v3:
time: 69.9 us; the launch traced here: 69.8 us
  Pallas kernels  67.5 us (97%)
  local copies, waits for them, and re-layouts  1.59 us (2%)
    pallas_call x1, Pallas kernels, body(): pl.pallas_call(mega_kernel, out_shape=jax.ShapeDtypeStruct((16, 5120), BF...  67.5 us
    unnamed x1, local copies, waits for them, and re-layouts  1.59 us

profile of v3, /device:TPU:70, one launch (start us, length us, event | category | flops | bytes accessed | tf_op | source)
XLA Modules:
  0.0 69.8 jit_solution(10177293846995238227)
XLA Ops:
  0.7 67.5 %block_sparse_attention.1 = bf16[16,5120]{1,0:T(8,128)(2,1)} custom-call(bf16[16,5120]{1,0:T(8,128)(2,1)} %q_ref.1, bf16[16,5120]{1,0:T(8,128)(2,1)} %k_ref.1, bf16[16,5120]{1,0:T(8,128)(2,1)} %v_ref.1, s32[1,12]{1,0:T(1,128)} %lists_ref.1, s32[1]{0:T(128)S(6)} %copy.10.counts_ref, bf16[160,640]{1,0:T(8,128)(2,1)} %bitcast.3, f32[1,5120]{1,0:T(1,128)} %bitcast.4, ...), custom_call_target="tpu_custom_call" | custom-call | tf_op jit(solution)/shard_map/block_sparse_attention/pallas_call | solution.py:489
  68.2 1.6 %copy.11 = bf16[16,5120]{1,0:T(8,128)(2,1)} copy(bf16[16,5120]{1,0:T(8,128)(2,1)} %block_sparse_attention.1) | data formatting | bytes 327680

commit v4 on v3

--- a/solution.py
+++ b/solution.py
@@ -246,7 +246,7 @@
 
     def c_place(zi, l):
         zt = (z_base + zi) % 8
-        xd = jnp.where(j_mine < 4, row, half * 2 + l)
+        xd = jnp.where(j_mine < 4, (row + 2 * (zt % 2)) % 4, half * 2 + l)
         return zt, xd, (zt == z) & (xd == x)
 
     def item_scores(zi, l, n):
@@ -256,33 +256,32 @@
             [qbuf[l, zi].reshape(64, 128), qbuf[l + 2, zi].reshape(64, 128)], axis=0
         )
         blocks = [lsm[l, zq, 0, s] for s in range(SLOTS)]
+        right = lax.broadcasted_iota(jnp.int32, (1, 256), 1) // 128
         top = None
-        for s in range(SLOTS):
+        for s in range(0, SLOTS, 2):
             part = lax.dot_general(
-                q, rows_of(blocks[s], 0), (((1,), (1,)), ((), ())), preferred_element_type=F32
+                q, pair_of(blocks, s, 0), (((1,), (1,)), ((), ())), preferred_element_type=F32
             )
             if s >= FEWEST:
-                part = jnp.where(s < count, part, -1e30)
-            sc[n, s] = part
+                part = jnp.where(right + s < count, part, -1e30)
+            sc[n, s // 2] = part
             top = part if top is None else jnp.maximum(top, part)
         return blocks, jnp.max(top, axis=1, keepdims=True)
 
     def item_values(zi, l, n, blocks, top):
-        den = jnp.zeros((128, 128), F32)
+        den = jnp.zeros((128, 256), F32)
         mixed = jnp.zeros((128, 128), F32)
         for s in range(0, SLOTS, 2):
-            pair = []
-            for t in (s, s + 1):
-                p = jnp.exp2((sc[n, t] - top) * scale)
-                den = den + p
-                pair.append(p.astype(BF16))
+            p = jnp.exp2((sc[n, s // 2] - top) * scale)
+            den = den + p
             mixed = mixed + jnp.dot(
-                jnp.concatenate(pair, axis=1),
-                jnp.concatenate([rows_of(blocks[s], 1), rows_of(blocks[s + 1], 1)], axis=0),
-                preferred_element_type=F32,
+                p.astype(BF16), pair_of(blocks, s, 1), preferred_element_type=F32
             )
         den = jnp.sum(den, axis=1, keepdims=True)
         att[zi, l] = (mixed / den).astype(BF16)
+
+    def pair_of(blocks, s, which):
+        return jnp.concatenate([rows_of(blocks[s], which), rows_of(blocks[s + 1], which)], axis=0)
 
     def rows_of(kb, which):
         return jnp.concatenate(
@@ -325,7 +324,7 @@
 
     def relay(l, k):
         if k < 2:
-            relay_one(l, 5 * k + x, k)
+            relay_one(l, 5 * k + (x + 2 * (z % 2)) % 4, k)
         else:
             @pl.when(xl == l)
             def _():
@@ -333,7 +332,7 @@
 
     def relayed(l):
         for h in range(10):
-            source = h % 5 if h % 5 < 4 else (h // 5) * 2 + l
+            source = (h % 5 + 2 * (z % 2)) % 4 if h % 5 < 4 else (h // 5) * 2 + l
 
             @pl.when(x != source)
             def _(h=h):
@@ -502,7 +501,7 @@
             vm((4, 4, 4, 16, 128), BF16),
             vm((2, 8, 1, 128), jnp.int32),
             pltpu.SMEM((2, 8, 1, 128), jnp.int32),
-            vm((2, SLOTS, 128, 128), F32),
+            vm((2, SLOTS // 2, 128, 256), F32),
             vm((4, 2, 128, 128), BF16),
             vm((2, 10, 128, 128), BF16),
             vm((2, 8, 160, 640), BF16),

time: 69.9 us -> 69.9 us (level)
  no operation moved by 1% of the time
where the time goes in v4:
time: 69.9 us; the launch traced here: 69.7 us
  Pallas kernels  67.5 us (97%)
  local copies, waits for them, and re-layouts  1.59 us (2%)
    pallas_call x1, Pallas kernels, body(): pl.pallas_call(mega_kernel, out_shape=jax.ShapeDtypeStruct((16, 5120), BF...  67.5 us
    unnamed x1, local copies, waits for them, and re-layouts  1.59 us

profile of v4, /device:TPU:70, one launch (start us, length us, event | category | flops | bytes accessed | tf_op | source)
XLA Modules:
  0.0 69.7 jit_solution(12120774664934606293)
XLA Ops:
  0.7 67.5 %block_sparse_attention.1 = bf16[16,5120]{1,0:T(8,128)(2,1)} custom-call(bf16[16,5120]{1,0:T(8,128)(2,1)} %q_ref.1, bf16[16,5120]{1,0:T(8,128)(2,1)} %k_ref.1, bf16[16,5120]{1,0:T(8,128)(2,1)} %v_ref.1, s32[1,12]{1,0:T(1,128)} %lists_ref.1, s32[1]{0:T(128)S(6)} %copy.10.counts_ref, bf16[160,640]{1,0:T(8,128)(2,1)} %bitcast.3, f32[1,5120]{1,0:T(1,128)} %bitcast.4, ...), custom_call_target="tpu_custom_call" | custom-call | tf_op jit(solution)/shard_map/block_sparse_attention/pallas_call | solution.py:488
  68.2 1.6 %copy.11 = bf16[16,5120]{1,0:T(8,128)(2,1)} copy(bf16[16,5120]{1,0:T(8,128)(2,1)} %block_sparse_attention.1) | data formatting | bytes 327680
